TPU v7x, 256 devices: a whole 4x4x8 slice. The times are simulated.
256 devices in a mesh: kv: 8 (over z), roll: 32 (over x, y, core).
Axes of the slice: x: 4, y: 4, z: 8, core: 2. Of those that a mesh axis runs over, the one named last changes fastest.
Arguments:
- q_tokens: bfloat16 [1024, 24, 8192], P('roll', 'kv'), may hold values from -6 to 6
- grad_tokens: bfloat16 [1024, 24, 8192], P('roll', 'kv'), may hold values from -6 to 6
- roll_keys: bfloat16 [1024, 24, 1024], P('roll', 'kv'), may hold values from -6 to 6
- roll_values: bfloat16 [1024, 24, 1024], P('roll', 'kv'), may hold values from -6 to 6
- prompt_keys: bfloat16 [65536, 1024], P('roll', 'kv'), may hold values from -6 to 6
- prompt_values: bfloat16 [65536, 1024], P('roll', 'kv'), may hold values from -6 to 6
- slot_prompt: int32 [1024], replicated, may hold values from -1 to 31, as said below
- prompt_owner: int32 [32], replicated, may hold values from 0 to 31, each once
- roll_len: int32 [1024], replicated, may hold values from 1 to 24, as said below
- prompt_len: int32 [32], replicated, may hold values from 512 to 2048, as said below
Outputs:
- grad_query: bfloat16 [1024, 24, 8192], P('roll', 'kv')
- grad_roll_keys: bfloat16 [1024, 24, 1024], P('roll', 'kv')
- grad_roll_values: bfloat16 [1024, 24, 1024], P('roll', 'kv')
- grad_prompt_keys: bfloat16 [65536, 1024], P('roll', 'kv')
- grad_prompt_values: bfloat16 [65536, 1024], P('roll', 'kv')
Inputs may be any that keep to these rules, and one draw needn't show every extreme that they name: `slot_prompt`: entry n names the prompt of the rollout in slot n, or -1 for an empty slot. Slots d * 32 to d * 32 + 31 belong to index d of roll, live slots first. Every prompt has exactly 16 rollouts; an index of roll holds 0 to 32 rollouts and at most 2 of one prompt; some index holds 32, and some index holds 2 of one prompt. `prompt_owner`: each index of roll holds exactly one prompt. `roll_len`: some slot has 24. `prompt_len`: some prompt has 2048.
All inputs are finite; a program needn't handle non-finite values.
Results may differ from a plain program's by a relative error of at most 0.008.
Values may be sent and summed in bfloat16 or wider, within the bound.
A program may use at most 128 MiB of HBM per device.

v0:
```python
import jax
import jax.numpy as jnp
from jax import lax
from jax.sharding import PartitionSpec as P

HD = 128
GROUP = 16


def slot_tables(slot_prompt, prompt_owner, roll_count, slot_count, bucket_cap, my_index):
    own_prompt = lax.dynamic_slice_in_dim(slot_prompt, my_index * slot_count, slot_count)
    is_live = own_prompt >= 0
    numbers = jnp.arange(roll_count, dtype=jnp.int32)
    target = jnp.sum(
        jnp.where(own_prompt[:, None] == numbers[None, :], prompt_owner[None, :], 0), axis=1
    )
    slot_ids = jnp.arange(slot_count, dtype=jnp.int32)
    earlier = (own_prompt[None, :] == own_prompt[:, None]) & (slot_ids[None, :] < slot_ids[:, None])
    rank_in = jnp.sum(earlier.astype(jnp.int32), axis=1)
    bucket_at = jnp.where(is_live, target * bucket_cap + rank_in, -1)
    buckets = jnp.arange(roll_count * bucket_cap, dtype=jnp.int32)
    matches = bucket_at[None, :] == buckets[:, None]
    source = jnp.sum(jnp.where(matches, slot_ids[None, :], 0), axis=1)
    filled = jnp.any(matches, axis=1)
    return (bucket_at, is_live, source, filled)


def owner_tables(
    slot_prompt,
    prompt_owner,
    roll_len,
    prompt_len,
    roll_count,
    slot_count,
    bucket_cap,
    my_index,
    group_size,
):
    numbers = jnp.arange(roll_count, dtype=jnp.int32)
    my_prompt = jnp.sum(jnp.where(prompt_owner == my_index, numbers, 0))
    plen_live = jnp.sum(jnp.where(numbers == my_prompt, prompt_len, 0))
    all_slots = jnp.arange(slot_prompt.shape[0], dtype=jnp.int32)
    member = slot_prompt == my_prompt
    counted = jnp.cumsum(member.astype(jnp.int32)) - 1
    ordinal = jnp.arange(group_size, dtype=jnp.int32)
    chosen = member[None, :] & (counted[None, :] == ordinal[:, None])
    picked = jnp.sum(jnp.where(chosen, all_slots[None, :], 0), axis=1)
    device = picked // slot_count
    before = (
        member[None, :]
        & (all_slots[None, :] // slot_count == device[:, None])
        & (all_slots[None, :] < picked[:, None])
    )
    arrival = device * bucket_cap + jnp.sum(before.astype(jnp.int32), axis=1)
    lengths = jnp.sum(jnp.where(chosen, roll_len[None, :], 0), axis=1)
    return (arrival, lengths, plen_live)


def pack_rows(values, source, filled):
    fetched = jnp.take(values, source, axis=0)
    return jnp.where(filled[:, None, None], fetched, jnp.zeros((), values.dtype))


def unpack_rows(values, bucket_at, is_live):
    fetched = jnp.take(values, jnp.maximum(bucket_at, 0), axis=0)
    return jnp.where(is_live[:, None, None], fetched, jnp.zeros((), values.dtype))


def owner_work(q_in, g_in, k_in, v_in, keys, values, arrival, lengths, plen_live, group_size):
    softmax_scale = HD ** (-0.5)
    rows = q_in.shape[1]
    kv_local = keys.shape[1] // HD
    heads_per = q_in.shape[2] // (kv_local * HD)
    plen = keys.shape[0]
    per_block = max(1, min(group_size, 512 // (rows * kv_local * heads_per)))
    while group_size % per_block != 0:
        per_block = per_block - 1
    blocks = group_size // per_block
    tok_pos = jnp.arange(rows, dtype=jnp.int32)
    valid = tok_pos[None, :] < lengths[:, None]
    query = jnp.take(q_in, arrival, axis=0).reshape(
        blocks, per_block, rows, kv_local, heads_per, HD
    )
    grad_rows = jnp.take(g_in, arrival, axis=0)
    grads = jnp.where(valid[:, :, None], grad_rows, jnp.zeros((), grad_rows.dtype)).reshape(
        blocks, per_block, rows, kv_local, heads_per, HD
    )
    own_keys = jnp.take(k_in, arrival, axis=0).reshape(blocks, per_block, rows, kv_local, HD)
    own_values = jnp.take(v_in, arrival, axis=0).reshape(blocks, per_block, rows, kv_local, HD)
    pkeys = keys.reshape(plen, kv_local, HD)
    pvalues = values.reshape(plen, kv_local, HD)
    visible = (jnp.arange(plen, dtype=jnp.int32) < plen_live)[None, None, None, None, :]
    causal = (tok_pos[None, :] <= tok_pos[:, None])[None, :, None, None, :]
    f32 = jnp.float32

    def step(carry, inputs):
        acc_keys, acc_values = carry
        query_b, grads_b, okeys_b, ovalues_b = inputs
        prompt_scores = (
            jnp.einsum("ntkjd,pkd->ntkjp", query_b, pkeys, preferred_element_type=f32)
            * softmax_scale
        )
        local_scores = (
            jnp.einsum("ntkjd,nukd->ntkju", query_b, okeys_b, preferred_element_type=f32)
            * softmax_scale
        )
        row_max = jnp.maximum(
            jnp.max(jnp.where(visible, prompt_scores, -jnp.inf), axis=-1),
            jnp.max(jnp.where(causal, local_scores, -jnp.inf), axis=-1),
        )
        prompt_exp = jnp.where(visible, jnp.exp(prompt_scores - row_max[..., None]), 0.0)
        local_exp = jnp.where(causal, jnp.exp(local_scores - row_max[..., None]), 0.0)
        total = jnp.sum(prompt_exp, axis=-1) + jnp.sum(local_exp, axis=-1)
        prompt_probs = prompt_exp / total[..., None]
        local_probs = local_exp / total[..., None]
        prompt_dprobs = jnp.einsum("ntkjd,pkd->ntkjp", grads_b, pvalues, preferred_element_type=f32)
        local_dprobs = jnp.einsum(
            "ntkjd,nukd->ntkju", grads_b, ovalues_b, preferred_element_type=f32
        )
        delta = jnp.sum(prompt_probs * prompt_dprobs, axis=-1) + jnp.sum(
            local_probs * local_dprobs, axis=-1
        )
        prompt_ds = (prompt_probs * (prompt_dprobs - delta[..., None])).astype(jnp.bfloat16)
        local_ds = (local_probs * (local_dprobs - delta[..., None])).astype(jnp.bfloat16)
        prompt_half = prompt_probs.astype(jnp.bfloat16)
        local_half = local_probs.astype(jnp.bfloat16)
        grad_q = softmax_scale * (
            jnp.einsum("ntkjp,pkd->ntkjd", prompt_ds, pkeys, preferred_element_type=f32)
            + jnp.einsum("ntkju,nukd->ntkjd", local_ds, okeys_b, preferred_element_type=f32)
        )
        acc_keys = acc_keys + softmax_scale * jnp.einsum(
            "ntkjp,ntkjd->pkd", prompt_ds, query_b, preferred_element_type=f32
        )
        acc_values = acc_values + jnp.einsum(
            "ntkjp,ntkjd->pkd", prompt_half, grads_b, preferred_element_type=f32
        )
        grad_okeys = softmax_scale * jnp.einsum(
            "ntkju,ntkjd->nukd", local_ds, query_b, preferred_element_type=f32
        )
        grad_ovalues = jnp.einsum(
            "ntkju,ntkjd->nukd", local_half, grads_b, preferred_element_type=f32
        )
        return (
            (acc_keys, acc_values),
            (
                grad_q.astype(jnp.bfloat16),
                grad_okeys.astype(jnp.bfloat16),
                grad_ovalues.astype(jnp.bfloat16),
            ),
        )

    zeros_acc = jnp.zeros((plen, kv_local, HD), jnp.float32)
    (acc_keys, acc_values), (grad_q, grad_okeys, grad_ovalues) = lax.scan(
        step, (zeros_acc, zeros_acc), (query, grads, own_keys, own_values)
    )
    bucket_rows = q_in.shape[0]
    grad_q = grad_q.reshape(group_size, rows, q_in.shape[2])
    grad_okeys = grad_okeys.reshape(group_size, rows, k_in.shape[2])
    grad_ovalues = grad_ovalues.reshape(group_size, rows, k_in.shape[2])
    q_back = jnp.zeros((bucket_rows, rows, q_in.shape[2]), jnp.bfloat16).at[arrival].set(grad_q)
    k_back = jnp.zeros((bucket_rows, rows, k_in.shape[2]), jnp.bfloat16).at[arrival].set(grad_okeys)
    v_back = (
        jnp.zeros((bucket_rows, rows, k_in.shape[2]), jnp.bfloat16).at[arrival].set(grad_ovalues)
    )
    return (
        q_back,
        k_back,
        v_back,
        acc_keys.reshape(plen, -1).astype(jnp.bfloat16),
        acc_values.reshape(plen, -1).astype(jnp.bfloat16),
    )


def per_device(
    q_tokens,
    grad_tokens,
    roll_keys,
    roll_values,
    prompt_keys,
    prompt_values,
    slot_prompt,
    prompt_owner,
    roll_len,
    prompt_len,
):
    roll_count = lax.axis_size("roll")
    my_index = lax.axis_index("roll")
    slot_count = q_tokens.shape[0]
    bucket_cap = 2 * ((slot_count // 2 + roll_count - 1) // roll_count)
    bucket_at, is_live, source, filled = slot_tables(
        slot_prompt, prompt_owner, roll_count, slot_count, bucket_cap, my_index
    )
    arrival, lengths, plen_live = owner_tables(
        slot_prompt,
        prompt_owner,
        roll_len,
        prompt_len,
        roll_count,
        slot_count,
        bucket_cap,
        my_index,
        GROUP,
    )
    q_head, g_head, k_head, v_head = (
        lax.all_to_all(q_tokens, "kv", split_axis=2, concat_axis=1, tiled=True),
        lax.all_to_all(grad_tokens, "kv", split_axis=2, concat_axis=1, tiled=True),
        lax.all_to_all(roll_keys, "kv", split_axis=2, concat_axis=1, tiled=True),
        lax.all_to_all(roll_values, "kv", split_axis=2, concat_axis=1, tiled=True),
    )
    sent_q = pack_rows(q_head, source, filled)
    sent_g = pack_rows(g_head, source, filled)
    sent_k = pack_rows(k_head, source, filled)
    sent_v = pack_rows(v_head, source, filled)
    q_in, g_in, k_in, v_in = (
        lax.all_to_all(sent_q, "roll", split_axis=0, concat_axis=0, tiled=True),
        lax.all_to_all(sent_g, "roll", split_axis=0, concat_axis=0, tiled=True),
        lax.all_to_all(sent_k, "roll", split_axis=0, concat_axis=0, tiled=True),
        lax.all_to_all(sent_v, "roll", split_axis=0, concat_axis=0, tiled=True),
    )
    q_back, k_back, v_back, grad_pkeys, grad_pvalues = owner_work(
        q_in, g_in, k_in, v_in, prompt_keys, prompt_values, arrival, lengths, plen_live, GROUP
    )
    q_home, k_home, v_home = (
        lax.all_to_all(q_back, "roll", split_axis=0, concat_axis=0, tiled=True),
        lax.all_to_all(k_back, "roll", split_axis=0, concat_axis=0, tiled=True),
        lax.all_to_all(v_back, "roll", split_axis=0, concat_axis=0, tiled=True),
    )
    slot_q = unpack_rows(q_home, bucket_at, is_live)
    slot_k = unpack_rows(k_home, bucket_at, is_live)
    slot_v = unpack_rows(v_home, bucket_at, is_live)
    grad_query, grad_okeys, grad_ovalues = (
        lax.all_to_all(slot_q, "kv", split_axis=1, concat_axis=2, tiled=True),
        lax.all_to_all(slot_k, "kv", split_axis=1, concat_axis=2, tiled=True),
        lax.all_to_all(slot_v, "kv", split_axis=1, concat_axis=2, tiled=True),
    )
    return (grad_query, grad_okeys, grad_ovalues, grad_pkeys, grad_pvalues)


def solution(mesh):
    in_specs = (
        P("roll", "kv", None),
        P("roll", "kv", None),
        P("roll", "kv", None),
        P("roll", "kv", None),
        P("roll", "kv"),
        P("roll", "kv"),
        P(),
        P(),
        P(),
        P(),
    )
    out_specs = (
        P("roll", "kv", None),
        P("roll", "kv", None),
        P("roll", "kv", None),
        P("roll", "kv"),
        P("roll", "kv"),
    )
    return jax.shard_map(
        per_device, mesh=mesh, in_specs=in_specs, out_specs=out_specs, check_vma=False
    )
```

profile of v0, /device:TPU:1, one launch (start us, length us, event | category | flops | bytes accessed | tf_op | source)
XLA Modules:
  0.0 749.0 jit_solution(18230704073962808480)
XLA Ops:
  3.7 9.0 %all-to-all-start.2 = ((bf16[8,2,6144]{2,1,0:T(2,128)(2,1)}), bf16[8,2,6144]{2,1,0:T(2,128)(2,1)S(1)}, u32[]{:S(2)}, u32[]{:S(2)}) async-start(bf16[8,2,6144]{2,1,0:T(2,128)(2,1)} %reshape.568), calls=%async_computation.2 | async-start | bytes 393216 | tf_op jit(solution)/shard_map/all_to_all | solution.py:207
  15.7 5.8 all-to-all-done.2
  25.0 8.4 %copy.210 = bf16[32,3,8192]{0,1,2:T(4,128)(2,1)} copy(bf16[32,3,8192]{2,0,1:T(8,128)(2,1)S(1)} %copy-done.10) | data formatting | bytes 3145728 | tf_op args[0]
  33.4 9.8 %reshape.566 = bf16[8,2,49152]{2,1,0:T(2,128)(2,1)} reshape(bf16[8192,3,32]{2,1,0:T(4,128)(2,1)} %bitcast.397) | data formatting | bytes 3145728
  43.1 6.7 all-to-all-start
  49.8 8.4 %copy.218 = bf16[32,3,8192]{0,1,2:T(4,128)(2,1)} copy(bf16[32,3,8192]{2,0,1:T(8,128)(2,1)S(1)} %copy-done.11) | data formatting | bytes 3145728 | tf_op args[1]
  58.2 9.8 %reshape.570 = bf16[8,2,49152]{2,1,0:T(2,128)(2,1)} reshape(bf16[8192,3,32]{2,1,0:T(4,128)(2,1)} %bitcast.398) | data formatting | bytes 3145728
  68.0 20.4 %all-to-all-done = bf16[8,2,49152]{2,1,0:T(2,128)(2,1)S(1)} async-done(((bf16[8,2,49152]{2,1,0:T(2,128)(2,1)}), bf16[8,2,49152]{2,1,0:T(2,128)(2,1)S(1)}, u32[]{:S(2)}, u32[]{:S(2)}) %all-to-all-start) | async-done | bytes 1572896 | tf_op jit(solution)/shard_map/all_to_all | solution.py:205
  108.1 22.0 %all-to-all-done.4 = bf16[8,2,49152]{2,1,0:T(2,128)(2,1)S(1)} async-done(((bf16[8,2,49152]{2,1,0:T(2,128)(2,1)}), bf16[8,2,49152]{2,1,0:T(2,128)(2,1)S(1)}, u32[]{:S(2)}, u32[]{:S(2)}) %all-to-all-start.4) | async-done | bytes 1572896 | tf_op jit(solution)/shard_map/all_to_all | solution.py:206
  130.2 9.8 %all-to-all-start.3 = ((bf16[64,24,128]{2,1,0:T(8,128)(2,1)}), bf16[64,24,128]{2,1,0:T(8,128)(2,1)S(1)}, u32[]{:S(2)}, u32[]{:S(2)}) async-start(bf16[64,24,128]{2,1,0:T(8,128)(2,1)} %get-tuple-element.304), calls=%async_computation.3 | async-start | bytes 786432 | tf_op jit(solution)/shard_map/all_to_all | solution.py:217
  139.9 7.6 %reshape.567 = bf16[8192,3,32]{2,1,0:T(4,128)(2,1)} reshape(bf16[8,2,49152]{2,1,0:T(2,128)(2,1)S(1)} %all-to-all-done) | data formatting | bytes 3145728
  147.6 11.8 %copy.249 = bf16[32,3,8,1024]{3,0,1,2:T(8,128)(2,1)} copy(bf16[32,3,8,1024]{0,1,3,2:T(4,128)(2,1)} %bitcast.395) | data formatting | bytes 3145728 | tf_op jit(solution)/shard_map/all_to_all | solution.py:205
  164.2 7.6 %reshape.571 = bf16[8192,3,32]{2,1,0:T(4,128)(2,1)} reshape(bf16[8,2,49152]{2,1,0:T(2,128)(2,1)S(1)} %all-to-all-done.4) | data formatting | bytes 3145728
  171.8 10.5 %copy.253 = bf16[32,3,8,1024]{3,0,1,2:T(8,128)(2,1)S(1)} copy(bf16[32,3,8,1024]{0,1,3,2:T(4,128)(2,1)} %bitcast.396) | data formatting | bytes 3145728 | tf_op jit(solution)/shard_map/all_to_all | solution.py:206
  185.6 7.4 all-to-all-start.7
  193.1 4.5 select_select_fusion
  197.5 5.9 all-to-all-done.7
  203.4 42.8 %all_to_all.161 = bf16[64,24,1024]{2,1,0:T(8,128)(2,1)} all-to-all(bf16[64,24,1024]{2,1,0:T(8,128)(2,1)S(1)} %get-tuple-element.306), channel_id=1, replica_groups=mesh['kv'=8,'roll'=32] {'roll'}, dimensions={0} | all-to-all | bytes 6291456 | tf_op jit(solution)/shard_map/all_to_all | solution.py:215
  246.2 4.3 all-to-all-start.5
  265.2 25.1 %all-to-all-done.5 = bf16[64,24,1024]{2,1,0:T(8,128)(2,1)S(1)} async-done(((bf16[64,24,1024]{2,1,0:T(8,128)(2,1)}), bf16[64,24,1024]{2,1,0:T(8,128)(2,1)S(1)}, u32[]{:S(2)}, u32[]{:S(2)}) %all-to-all-start.5) | async-done | bytes 3145760 | tf_op jit(solution)/shard_map/all_to_all | solution.py:216
  293.7 306.5 %while.20 = (s32[]{:T(128)}, f32[2048,1,128]{0,2,1:T(8,128)}, f32[2048,1,128]{0,2,1:T(8,128)}, bf16[8,2,24,1,8,128]{5,4,2,1,3,0:T(8,128)(2,1)}, bf16[8,2,24,1,12...) while((s32[]{:T(128)}, f32[2048,1,128]{0,2,1:T(8,128)}, ...), condition=%wide.region_18.23_spmd.clone.clone, body=%wide.region_11.22_spmd.clone.clone.sunk | while | flops 1036588480 | bytes 63572484 | solution.py:153
  308.5 4.2 fusion.112
  383.8 4.2 fusion.112
  460.9 4.2 fusion.112
  499.4 4.2 fusion.112
  538.0 4.2 fusion.112
  603.8 5.0 all-to-all-start.10
  612.4 6.8 all-to-all-done.10
  624.1 8.9 %all-to-all-done.12 = bf16[64,24,128]{2,1,0:T(8,128)(2,1)S(1)} async-done(((bf16[64,24,128]{2,1,0:T(8,128)(2,1)}), bf16[64,24,128]{2,1,0:T(8,128)(2,1)S(1)}, u32[]{:S(2)}, u32[]{:S(2)}) %all-to-all-start.12) | async-done | bytes 393248 | tf_op jit(solution)/shard_map/all_to_all | solution.py:226
  643.0 5.7 all-to-all-done.13
  653.6 39.2 %all-to-all-done.8 = bf16[64,24,1024]{2,1,0:T(8,128)(2,1)S(1)} async-done(((bf16[64,24,1024]{2,1,0:T(8,128)(2,1)}), bf16[64,24,1024]{2,1,0:T(8,128)(2,1)S(1)}, u32[]{:S(2)}, u32[]{:S(2)}) %all-to-all-start.8) | async-done | bytes 3145760 | tf_op jit(solution)/shard_map/all_to_all | solution.py:224
  714.1 33.6 %all-to-all-done.9 = bf16[32,24,1024]{2,0,1:T(8,128)(2,1)S(1)} async-done(((bf16[32,24,1024]{2,0,1:T(8,128)(2,1)}), bf16[32,24,1024]{2,0,1:T(8,128)(2,1)S(1)}, u32[]{:S(2)}, u32[]{:S(2)}) %all-to-all-start.9) | async-done | bytes 1572896 | tf_op jit(solution)/shard_map/all_to_all | solution.py:232
  (567 shorter events, 389.0 us)
Async XLA Ops:
  0.6 24.3 %copy-start.10 = (bf16[32,3,8192]{2,0,1:T(8,128)(2,1)S(1)}, bf16[32,3,8192]{2,0,1:T(8,128)(2,1)}, u32[]{:S(2)}) copy-start(bf16[32,3,8192]{2,0,1:T(8,128)(2,1)} %param.22) | copy-start | bytes 4718596
  3.7 17.8 %all-to-all-start.2 = ((bf16[8,2,6144]{2,1,0:T(2,128)(2,1)}), bf16[8,2,6144]{2,1,0:T(2,128)(2,1)S(1)}, u32[]{:S(2)}, u32[]{:S(2)}) async-start(bf16[8,2,6144]{2,1,0:T(2,128)(2,1)} %reshape.568), calls=%async_computation.2 | async-start | bytes 393216 | tf_op jit(solution)/shard_map/all_to_all | solution.py:207
  21.6 21.6 %all-to-all-start.6 = ((bf16[8,2,6144]{2,1,0:T(2,128)(2,1)}), bf16[8,2,6144]{2,1,0:T(2,128)(2,1)S(1)}, u32[]{:S(2)}, u32[]{:S(2)}) async-start(bf16[8,2,6144]{2,1,0:T(2,128)(2,1)} %reshape.572), calls=%async_computation.6 | async-start | bytes 393216 | tf_op jit(solution)/shard_map/all_to_all | solution.py:208
  43.1 45.3 %all-to-all-start = ((bf16[8,2,49152]{2,1,0:T(2,128)(2,1)}), bf16[8,2,49152]{2,1,0:T(2,128)(2,1)S(1)}, u32[]{:S(2)}, u32[]{:S(2)}) async-start(bf16[8,2,49152]{2,1,0:T(2,128)(2,1)} %reshape.566), calls=%async_computation | async-start | bytes 3145728 | tf_op jit(solution)/shard_map/all_to_all | solution.py:205
  68.0 24.0 %copy-start.19 = (s32[1024]{0:T(1024)S(1)}, s32[1024]{0:T(1024)}, u32[]{:S(2)}) copy-start(s32[1024]{0:T(1024)} %param.28) | copy-start | bytes 12292
  68.0 24.7 %copy-start.23 = (s32[32]{0:T(128)S(1)}, s32[32]{0:T(128)}, u32[]{:S(2)}) copy-start(s32[32]{0:T(128)} %param.29) | copy-start | bytes 388
  88.4 41.7 %all-to-all-start.4 = ((bf16[8,2,49152]{2,1,0:T(2,128)(2,1)}), bf16[8,2,49152]{2,1,0:T(2,128)(2,1)S(1)}, u32[]{:S(2)}, u32[]{:S(2)}) async-start(bf16[8,2,49152]{2,1,0:T(2,128)(2,1)} %reshape.570), calls=%async_computation.4 | async-start | bytes 3145728 | tf_op jit(solution)/shard_map/all_to_all | solution.py:206
  130.2 55.5 %all-to-all-start.3 = ((bf16[64,24,128]{2,1,0:T(8,128)(2,1)}), bf16[64,24,128]{2,1,0:T(8,128)(2,1)S(1)}, u32[]{:S(2)}, u32[]{:S(2)}) async-start(bf16[64,24,128]{2,1,0:T(8,128)(2,1)} %get-tuple-element.304), calls=%async_computation.3 | async-start | bytes 786432 | tf_op jit(solution)/shard_map/all_to_all | solution.py:217
  185.6 17.8 %all-to-all-start.7 = ((bf16[64,24,128]{2,1,0:T(8,128)(2,1)}), bf16[64,24,128]{2,1,0:T(8,128)(2,1)}, u32[]{:S(2)}, u32[]{:S(2)}) async-start(bf16[64,24,128]{2,1,0:T(8,128)(2,1)} %get-tuple-element.303), calls=%async_computation.7 | async-start | bytes 786432 | tf_op jit(solution)/shard_map/all_to_all | solution.py:218
  246.2 44.0 %all-to-all-start.5 = ((bf16[64,24,1024]{2,1,0:T(8,128)(2,1)}), bf16[64,24,1024]{2,1,0:T(8,128)(2,1)S(1)}, u32[]{:S(2)}, u32[]{:S(2)}) async-start(bf16[64,24,1024]{2,1,0:T(8,128)(2,1)} %get-tuple-element.305), calls=%async_computation.5 | async-start | bytes 6291456 | tf_op jit(solution)/shard_map/all_to_all | solution.py:216
  293.8 14.7 %copy-start.3 = (bf16[2,24,8,128]{3,2,1,0:T(8,128)(2,1)}, bf16[2,24,8,128]{3,2,1,0:T(8,128)(2,1)S(1)}, u32[]{:S(2)}) copy-start(bf16[2,24,8,128]{3,2,1,0:T(8,128)(2,1)S(1)} %get-tuple-element.407) | copy-start | bytes 294916 | tf_op jit(solution)/shard_map/while
  330.5 14.7 %copy-start.3 = (bf16[2,24,8,128]{3,2,1,0:T(8,128)(2,1)}, bf16[2,24,8,128]{3,2,1,0:T(8,128)(2,1)S(1)}, u32[]{:S(2)}) copy-start(bf16[2,24,8,128]{3,2,1,0:T(8,128)(2,1)S(1)} %get-tuple-element.407) | copy-start | bytes 294916 | tf_op jit(solution)/shard_map/while
  330.5 9.6 %copy-start.12 = (pred[24,24]{0,1:T(8,128)(4,1)}, pred[24,24]{0,1:T(8,128)(4,1)S(1)}, u32[]{:S(2)}) copy-start(pred[24,24]{0,1:T(8,128)(4,1)S(1)} %fusion.110) | copy-start | bytes 1732 | tf_op jit(solution)/shard_map/while
  369.0 14.7 %copy-start.3 = (bf16[2,24,8,128]{3,2,1,0:T(8,128)(2,1)}, bf16[2,24,8,128]{3,2,1,0:T(8,128)(2,1)S(1)}, u32[]{:S(2)}) copy-start(bf16[2,24,8,128]{3,2,1,0:T(8,128)(2,1)S(1)} %get-tuple-element.407) | copy-start | bytes 294916 | tf_op jit(solution)/shard_map/while
  369.1 9.6 %copy-start.12 = (pred[24,24]{0,1:T(8,128)(4,1)}, pred[24,24]{0,1:T(8,128)(4,1)S(1)}, u32[]{:S(2)}) copy-start(pred[24,24]{0,1:T(8,128)(4,1)S(1)} %fusion.110) | copy-start | bytes 1732 | tf_op jit(solution)/shard_map/while
  407.6 14.7 %copy-start.3 = (bf16[2,24,8,128]{3,2,1,0:T(8,128)(2,1)}, bf16[2,24,8,128]{3,2,1,0:T(8,128)(2,1)S(1)}, u32[]{:S(2)}) copy-start(bf16[2,24,8,128]{3,2,1,0:T(8,128)(2,1)S(1)} %get-tuple-element.407) | copy-start | bytes 294916 | tf_op jit(solution)/shard_map/while
  446.1 14.7 %copy-start.3 = (bf16[2,24,8,128]{3,2,1,0:T(8,128)(2,1)}, bf16[2,24,8,128]{3,2,1,0:T(8,128)(2,1)S(1)}, u32[]{:S(2)}) copy-start(bf16[2,24,8,128]{3,2,1,0:T(8,128)(2,1)S(1)} %get-tuple-element.407) | copy-start | bytes 294916 | tf_op jit(solution)/shard_map/while
  446.2 9.6 %copy-start.12 = (pred[24,24]{0,1:T(8,128)(4,1)}, pred[24,24]{0,1:T(8,128)(4,1)S(1)}, u32[]{:S(2)}) copy-start(pred[24,24]{0,1:T(8,128)(4,1)S(1)} %fusion.110) | copy-start | bytes 1732 | tf_op jit(solution)/shard_map/while
  484.7 14.7 %copy-start.3 = (bf16[2,24,8,128]{3,2,1,0:T(8,128)(2,1)}, bf16[2,24,8,128]{3,2,1,0:T(8,128)(2,1)S(1)}, u32[]{:S(2)}) copy-start(bf16[2,24,8,128]{3,2,1,0:T(8,128)(2,1)S(1)} %get-tuple-element.407) | copy-start | bytes 294916 | tf_op jit(solution)/shard_map/while
  484.7 9.6 %copy-start.12 = (pred[24,24]{0,1:T(8,128)(4,1)}, pred[24,24]{0,1:T(8,128)(4,1)S(1)}, u32[]{:S(2)}) copy-start(pred[24,24]{0,1:T(8,128)(4,1)S(1)} %fusion.110) | copy-start | bytes 1732 | tf_op jit(solution)/shard_map/while
  523.2 14.7 %copy-start.3 = (bf16[2,24,8,128]{3,2,1,0:T(8,128)(2,1)}, bf16[2,24,8,128]{3,2,1,0:T(8,128)(2,1)S(1)}, u32[]{:S(2)}) copy-start(bf16[2,24,8,128]{3,2,1,0:T(8,128)(2,1)S(1)} %get-tuple-element.407) | copy-start | bytes 294916 | tf_op jit(solution)/shard_map/while
  561.8 14.7 %copy-start.3 = (bf16[2,24,8,128]{3,2,1,0:T(8,128)(2,1)}, bf16[2,24,8,128]{3,2,1,0:T(8,128)(2,1)S(1)}, u32[]{:S(2)}) copy-start(bf16[2,24,8,128]{3,2,1,0:T(8,128)(2,1)S(1)} %get-tuple-element.407) | copy-start | bytes 294916 | tf_op jit(solution)/shard_map/while
  600.3 33.3 %copy-start.21 = (pred[32]{0:T(512)(128)(4,1)S(1)}, pred[32]{0:T(512)(128)(4,1)}, u32[]{:S(2)}) copy-start(pred[32]{0:T(512)(128)(4,1)} %get-tuple-element.283) | copy-start | bytes 100
  600.3 33.3 %copy-start.22 = (pred[32]{0:T(512)(128)(4,1)S(1)}, pred[32]{0:T(512)(128)(4,1)}, u32[]{:S(2)}) copy-start(pred[32]{0:T(512)(128)(4,1)} %get-tuple-element.281) | copy-start | bytes 100
  600.3 37.6 %copy-start.16 = (bf16[8,2,24,1,8,128]{5,4,2,1,3,0:T(8,128)(2,1)S(1)}, bf16[8,2,24,1,8,128]{5,4,2,1,3,0:T(8,128)(2,1)}, u32[]{:S(2)}) copy-start(bf16[8,2,24,1,8,128]{5,4,2,1,3,0:T(8,128)(2,1)} %get-tuple-element.89) | copy-start | bytes 2359300
  603.8 15.3 %all-to-all-start.10 = ((bf16[64,24,128]{2,1,0:T(8,128)(2,1)}), bf16[64,24,128]{2,1,0:T(8,128)(2,1)S(1)}, u32[]{:S(2)}, u32[]{:S(2)}) async-start(bf16[64,24,128]{2,1,0:T(8,128)(2,1)} %scatter_fusion.1), calls=%async_computation.10 | async-start | bytes 786432 | tf_op jit(solution)/shard_map/all_to_all | solution.py:225
  619.1 13.9 %all-to-all-start.12 = ((bf16[64,24,128]{2,1,0:T(8,128)(2,1)}), bf16[64,24,128]{2,1,0:T(8,128)(2,1)S(1)}, u32[]{:S(2)}, u32[]{:S(2)}) async-start(bf16[64,24,128]{2,1,0:T(8,128)(2,1)} %scatter_fusion.2), calls=%async_computation.12 | async-start | bytes 786432 | tf_op jit(solution)/shard_map/all_to_all | solution.py:226
  634.5 14.3 %all-to-all-start.13 = ((bf16[32,24,128]{2,0,1:T(8,128)(2,1)}), bf16[32,24,128]{2,0,1:T(8,128)(2,1)S(1)}, u32[]{:S(2)}, u32[]{:S(2)}) async-start(bf16[32,24,128]{2,0,1:T(8,128)(2,1)} %copy.234), calls=%async_computation.13 | async-start | bytes 393216 | tf_op jit(solution)/shard_map/all_to_all | solution.py:234
  648.8 44.0 %all-to-all-start.8 = ((bf16[64,24,1024]{2,1,0:T(8,128)(2,1)}), bf16[64,24,1024]{2,1,0:T(8,128)(2,1)S(1)}, u32[]{:S(2)}, u32[]{:S(2)}) async-start(bf16[64,24,1024]{2,1,0:T(8,128)(2,1)} %scatter_fusion), calls=%async_computation.8 | async-start | bytes 6291456 | tf_op jit(solution)/shard_map/all_to_all | solution.py:224
  692.8 13.0 %all-to-all-start.11 = ((bf16[32,24,128]{2,0,1:T(8,128)(2,1)}), bf16[32,24,128]{2,0,1:T(8,128)(2,1)S(1)}, u32[]{:S(2)}, u32[]{:S(2)}) async-start(bf16[32,24,128]{2,0,1:T(8,128)(2,1)} %copy.232), calls=%async_computation.11 | async-start | bytes 393216 | tf_op jit(solution)/shard_map/all_to_all | solution.py:233
  699.7 9.7 %copy-start.13 = (f32[2048,1,128]{0,2,1:T(8,128)S(1)}, f32[2048,1,128]{0,2,1:T(8,128)}, u32[]{:S(2)}) copy-start(f32[2048,1,128]{0,2,1:T(8,128)} %get-tuple-element.93) | copy-start | bytes 3145732
  705.8 41.8 %all-to-all-start.9 = ((bf16[32,24,1024]{2,0,1:T(8,128)(2,1)}), bf16[32,24,1024]{2,0,1:T(8,128)(2,1)S(1)}, u32[]{:S(2)}, u32[]{:S(2)}) async-start(bf16[32,24,1024]{2,0,1:T(8,128)(2,1)} %copy.230), calls=%async_computation.9 | async-start | bytes 3145728 | tf_op jit(solution)/shard_map/all_to_all | solution.py:232
  (112 other events, 397.0 us)
where the time goes:
time: 758 us; the launch traced here: 749 us
  local copies, waits for them, and re-layouts  203 us (27%)
  waiting for transfers between devices  178 us (23%)
  matrix products  155 us (20%)
  other arithmetic  101 us (13%)
  starting transfers between devices  67.3 us (9%)
  blocking collectives  42.8 us (6%)
    unnamed x36, local copies, waits for them, and re-layouts  61.5 us
    all_to_all x1, blocking collectives, per_device(): lax.all_to_all(sent_q, 'roll', split_axis=0, concat_axis=0, tiled=True)  42.8 us
    all_to_all x1, waiting for transfers between devices, per_device(): lax.all_to_all(q_back, 'roll', split_axis=0, concat_axis=0, tiled=True)  39.2 us
    another operation x21, other arithmetic  37.9 us
    all_to_all x1, waiting for transfers between devices, per_device(): lax.all_to_all(slot_q, 'kv', split_axis=1, concat_axis=2, tiled=True)  33.6 us
    dot_general x8, matrix products, step(): jnp.einsum('ntkjd,pkd->ntkjp', grads_b, pvalues, preferred_element_type=f32)  33.4 us
    dot_general x8, matrix products, step(): jnp.einsum('ntkjp,ntkjd->pkd', prompt_half, grads_b, preferred_element_ty...  25.7 us
    all_to_all x1, waiting for transfers between devices, per_device(): lax.all_to_all(sent_g, 'roll', split_axis=0, concat_axis=0, tiled=True)  25.1 us
  transfers between devices with their start and end apart: 13, of which 11 were waited for; matrix products, arithmetic and copies ran while one was open for 19% of the time, Pallas kernels for 0%

commit v1 on v0

--- a/solution.py
+++ b/solution.py
@@ -1,6 +1,8 @@
 import jax
 import jax.numpy as jnp
 from jax import lax
+from jax.experimental import pallas as pl
+from jax.experimental.pallas import tpu as pltpu
 from jax.sharding import PartitionSpec as P
 
 HD = 128
@@ -171,7 +173,7 @@
     )
 
 
-def per_device(
+def general(
     q_tokens,
     grad_tokens,
     roll_keys,
@@ -236,6 +238,686 @@
     return (grad_query, grad_okeys, grad_ovalues, grad_pkeys, grad_pvalues)
 
 
+CAP = 8
+N_KV = 8
+N_ROLL = 32
+SLOTS = 32
+TSLOTS = 1024
+RT = 24
+PLEN = 2048
+HG = 8
+ROWS = GROUP * RT
+MESH = pl.DeviceIdType.MESH
+BF = jnp.bfloat16
+F32 = jnp.float32
+CHUNK = 64
+LANES = CHUNK * HG
+KB = 256
+WIN = 2 * CHUNK
+LOG2E = 1.4426950408889634
+VMEM_BYTES = 56 * 1024 * 1024
+
+
+def dot(a, b):
+    return jnp.dot(a, b, preferred_element_type=F32)
+
+
+def route_tables(slot_prompt, prompt_owner, roll_len, prompt_len, me):
+    n = jnp.arange(TSLOTS, dtype=jnp.int32)
+    names = jnp.arange(N_ROLL, dtype=jnp.int32)
+    live = slot_prompt >= 0
+    dest = jnp.sum(
+        jnp.where(slot_prompt[:, None] == names[None, :], prompt_owner[None, :] + 1, 0), axis=1
+    ) - 1
+    src = n // SLOTS
+    xs, ys = src // 8, (src // 2) % 4
+    xd, yd, cd = dest // 8, (dest // 2) % 4, dest % 2
+    chip = xs * 4 + ys
+    keys = jnp.stack(
+        [
+            (chip * 2 + cd) * 4 + xd,
+            (chip * 2 + cd) * 4 + yd,
+            ((xd * 4 + ys) * 2 + cd) * 4 + yd,
+            ((xs * 4 + yd) * 2 + cd) * 4 + xd,
+            dest,
+        ]
+    )
+    keys = jnp.where(live[None, :], keys, -1)
+    same = (keys[:, None, :] == keys[:, :, None]) & (n[None, None, :] < n[None, :, None])
+    rank = jnp.sum(same.astype(jnp.int32), axis=2)
+    fits = jnp.max(jnp.where(live[None, :], rank[:4], 0)) < CAP
+
+    x, y, c = me // 8, (me // 2) % 4, me % 2
+    first = jnp.where((live & (cd == c))[None, :], jnp.stack([xd, yd]) * CAP + rank[:2], -1)
+    own = lax.dynamic_slice_in_dim(first, me * SLOTS, SLOTS, 1)
+    other = lax.dynamic_slice_in_dim(first, (me + 1 - 2 * c) * SLOTS, SLOTS, 1)
+    first = jnp.concatenate([own, other], axis=1)
+
+    mine = live & (dest == me)
+    in_a = live & (ys == y) & (xd == x) & (cd == c)
+    in_b = live & (xs == x) & (yd == y) & (cd == c)
+    pos = jnp.stack(
+        [
+            jnp.where(in_a, xs * CAP + rank[0], -1),
+            jnp.where(in_b, ys * CAP + rank[1], -1),
+            jnp.where(mine, ys * CAP + rank[2], -1),
+            jnp.where(mine, xs * CAP + rank[3], -1),
+            jnp.where(mine, rank[4], -1),
+        ]
+    )
+    val = jnp.stack([yd * CAP + rank[2], xd * CAP + rank[3], rank[4], rank[4], roll_len - 1])
+    places = jnp.arange(32, dtype=jnp.int32)
+    picked = jnp.sum(
+        jnp.where(pos[:, None, :] == places[None, :, None], val[:, None, :] + 1, 0), axis=2
+    ) - 1
+    lens = picked[4, :GROUP] + 1
+
+    def spread(code, h):
+        return jnp.where(code >= 0, (code // CAP) * 16 + h * CAP + code % CAP, -1)
+
+    second = picked[:2].reshape(2, 4, CAP)
+    second = jnp.stack([spread(second, 0), spread(second, 1)], axis=2).reshape(2, 64)
+    third = picked[2:4].reshape(2, 4, CAP)
+    third = jnp.stack([third, jnp.where(third >= 0, third + GROUP, -1)], axis=2).reshape(2, 64)
+    there = jnp.stack([first, second, third])
+    back = jnp.stack([spread(first, 0), spread(first, 1), second, third])
+    at = jnp.arange(64, dtype=jnp.int32)
+    mats = (there[:, :, None, :] == at[None, None, :, None]).astype(BF)
+    mats_back = (back[:, :, :, None] == at[None, None, None, :]).astype(BF)
+    my_prompt = prompt_owner == me
+    plen = jnp.sum(jnp.where(my_prompt, prompt_len, 0)).reshape(1)
+    return fits, mats, mats_back, lens, plen
+
+
+class Place:
+    def __init__(self):
+        self.kv = lax.axis_index("kv")
+        self.me = lax.axis_index("roll")
+        self.x = self.me // 8
+        self.y = (self.me // 2) % 4
+        self.c = self.me % 2
+
+    def pos(self, axis):
+        return self.x if axis == 0 else self.y
+
+    def chip(self, axis, step):
+        if axis == 0:
+            return (self.kv, ((self.x + step) % 4) * 8 + self.y * 2 + self.c)
+        return (self.kv, self.x * 8 + ((self.y + step) % 4) * 2 + self.c)
+
+    def core(self):
+        return (self.kv, self.x * 8 + self.y * 2 + 1 - self.c)
+
+    def head(self, step):
+        return ((self.kv + step) % N_KV, self.me)
+
+    def greet(self):
+        peers = [self.core()]
+        peers += [self.chip(axis, i) for axis in (0, 1) for i in (1, 2, 3)]
+        peers += [self.head(i) for i in range(1, N_KV)]
+        barrier = pltpu.get_barrier_semaphore()
+        for peer in peers:
+            pl.semaphore_signal(barrier, inc=1, device_id=peer, device_id_type=MESH)
+        pl.semaphore_wait(barrier, len(peers))
+
+
+def remote(src, dst, send, recv, peer):
+    return pltpu.make_async_remote_copy(
+        src_ref=src, dst_ref=dst, send_sem=send, recv_sem=recv, device_id=peer, device_id_type=MESH
+    )
+
+
+def rows16(p):
+    return pl.ds(pl.multiple_of(p * 16, 16), 16)
+
+
+def axis_send(place, axis, out, land, send, recv):
+    p = place.pos(axis)
+    copies = []
+    for i in (1, 2, 3):
+        q = (p + i) % 4
+        cp = remote(
+            out.at[rows16(q)], land.at[rows16(p)], send.at[i - 1], recv.at[i - 1],
+            place.chip(axis, i),
+        )
+        cp.start()
+        copies.append(cp)
+    land[rows16(p), :] = out[rows16(p), :]
+    return copies
+
+
+def axis_wait(place, axis, out, land, send, recv):
+    p = place.pos(axis)
+    for i in (1, 2, 3):
+        q = (p - i + 4) % 4
+        remote(
+            out.at[rows16(q)], land.at[rows16(q)], send.at[i - 1], recv.at[i - 1],
+            place.chip(axis, i),
+        ).wait_recv()
+
+
+def there_kernel(
+    q, g, k, v, mats, qk_out, gv_out,
+    cq, cg, ck, cv, s1, r1, s2, r2, s3,
+    core_s, core_r, p1_s, p1_r, p2_s, p2_r, z_s, z_r, loc,
+):
+    place = Place()
+    place.greet()
+    kv = place.kv
+    sent = []
+    pairs = ((q, cq), (k, ck), (g, cg), (v, cv))
+    arrived = []
+    for t in range(3):
+        group = []
+        for j, (a, b) in enumerate(pairs):
+            cp = remote(a.at[t], b.at[t], core_s.at[t, j], core_r.at[t, j], place.core())
+            cp.start()
+            group.append(cp)
+        arrived.append(group)
+        sent += group
+
+    def pack(t, h):
+        big, bigo, small, smallo = (q, cq, k, ck) if h == 0 else (g, cg, v, cv)
+        m = mats[0, h, :32, :]
+        dst = s1.at[h, t]
+
+        def put(a, b, lo, hi, at):
+            def one(o):
+                rows = jnp.concatenate([a[t, :, pl.ds(o, 512)], b[t, :, pl.ds(o, 512)]], axis=0)
+                return dot(m, rows).reshape(4, CAP, 512)
+
+            both = jnp.concatenate([one(lo), one(hi)], axis=1).reshape(64, 512)
+            dst[:, pl.ds(at, 512)] = both.astype(BF)
+
+        def body(i, _):
+            lo = pl.multiple_of(i * 512, 512)
+            put(big, bigo, lo, pl.multiple_of(lo + 4096, 512), lo)
+            return 0
+
+        lax.fori_loop(0, 8, body, 0)
+        put(small, smallo, 0, 512, 4096)
+
+    def turn(t, h):
+        m = mats[1, h]
+
+        def body(i, _):
+            lanes = pl.ds(pl.multiple_of(i * 512, 512), 512)
+            s2[h, t, :, lanes] = dot(m, r1[h, t, :, lanes]).astype(BF)
+            return 0
+
+        lax.fori_loop(0, 9, body, 0)
+
+    def finish(t, h):
+        m = mats[2, h, :32, :]
+
+        def body(i, _):
+            o = dot(m, r2[h, t, :, pl.ds(pl.multiple_of(i * 1024, 1024), 1024)]).astype(BF)
+            s3[h, t, i, :, 0:1024] = o[:16]
+            s3[h, t, i + 4, :, 0:1024] = o[16:]
+            return 0
+
+        lax.fori_loop(0, 4, body, 0)
+        o = dot(m, r2[h, t, :, 4096:4608]).astype(BF)
+        for i in range(4):
+            s3[h, t, i, :, 1024:1152] = o[:16, i * 128 : (i + 1) * 128]
+            s3[h, t, i + 4, :, 1024:1152] = o[16:, i * 128 : (i + 1) * 128]
+
+    def step1(t):
+        for j in range(4):
+            arrived[t][j].wait_recv()
+        for h in (0, 1):
+            pack(t, h)
+            sent.extend(axis_send(place, h, s1.at[h, t], r1.at[h, t], p1_s.at[h, t], p1_r.at[h, t]))
+
+    def step2(t):
+        for h in (0, 1):
+            axis_wait(place, h, s1.at[h, t], r1.at[h, t], p1_s.at[h, t], p1_r.at[h, t])
+            turn(t, h)
+            sent.extend(
+                axis_send(place, 1 - h, s2.at[h, t], r2.at[h, t], p2_s.at[h, t], p2_r.at[h, t])
+            )
+
+    local = []
+
+    def step3(t):
+        for h in (0, 1):
+            out = qk_out if h == 0 else gv_out
+            axis_wait(place, 1 - h, s2.at[h, t], r2.at[h, t], p2_s.at[h, t], p2_r.at[h, t])
+            finish(t, h)
+            for i in (4, 3, 5, 2, 6, 1, 7):
+                c = (kv + i) % N_KV
+                cp = remote(
+                    s3.at[h, t, c], out.at[3 * kv + t], z_s.at[h, t, i - 1], z_r.at[h, t, i - 1],
+                    place.head(i),
+                )
+                cp.start()
+                sent.append(cp)
+            cp = pltpu.make_async_copy(s3.at[h, t, kv], out.at[3 * kv + t], loc.at[h, t])
+            cp.start()
+            local.append(cp)
+
+    step1(0)
+    step1(1)
+    step2(0)
+    step1(2)
+    step2(1)
+    step3(0)
+    step2(2)
+    step3(1)
+    step3(2)
+    for t in range(3):
+        for h in (0, 1):
+            out = qk_out if h == 0 else gv_out
+            for i in range(1, N_KV):
+                c = (kv - i + N_KV) % N_KV
+                remote(
+                    s3.at[h, t, c], out.at[3 * c + t], z_s.at[h, t, i - 1], z_r.at[h, t, i - 1],
+                    place.head(i),
+                ).wait_recv()
+    for cp in local:
+        cp.wait()
+    for cp in sent:
+        cp.wait_send()
+
+
+def there(q, g, k, v, mats):
+    vm = pl.BlockSpec(memory_space=pltpu.VMEM)
+    hbm = pl.BlockSpec(memory_space=pl.ANY)
+    sem = pltpu.SemaphoreType.DMA
+    half = pltpu.VMEM((2, 3, 64, 4608), BF)
+    return pl.pallas_call(
+        there_kernel,
+        out_shape=[jax.ShapeDtypeStruct((RT, GROUP, 1152), BF)] * 2,
+        in_specs=[vm] * 5,
+        out_specs=[hbm] * 2,
+        scratch_shapes=[
+            pltpu.VMEM((3, SLOTS, 8192), BF),
+            pltpu.VMEM((3, SLOTS, 8192), BF),
+            pltpu.VMEM((3, SLOTS, 1024), BF),
+            pltpu.VMEM((3, SLOTS, 1024), BF),
+            half, half, half, half,
+            pltpu.VMEM((2, 3, N_KV, GROUP, 1152), BF),
+            sem((3, 4)), sem((3, 4)),
+            sem((2, 3, 3)), sem((2, 3, 3)),
+            sem((2, 3, 3)), sem((2, 3, 3)),
+            sem((2, 3, 7)), sem((2, 3, 7)),
+            sem((2, 3)),
+        ],
+        compiler_params=pltpu.CompilerParams(
+            collective_id=0, has_side_effects=True, vmem_limit_bytes=VMEM_BYTES
+        ),
+        name="there",
+    )(q, g, k, v, mats)
+
+
+def back_kernel(
+    d, mats, gq, gk, gv,
+    rz, s1, r1, s2, r2, own, snd, rcv,
+    z_s, z_r, p1_s, p1_r, p2_s, p2_r, core_s, core_r,
+):
+    place = Place()
+    place.greet()
+    kv = place.kv
+    sent = []
+    for t in range(3):
+        for i in (4, 3, 5, 2, 6, 1, 7):
+            c = (kv + i) % N_KV
+            cp = remote(
+                d.at[3 * c + t], rz.at[kv, t], z_s.at[t, i - 1], z_r.at[t, i - 1], place.head(i)
+            )
+            cp.start()
+            sent.append(cp)
+        rz[kv, t] = d[3 * kv + t]
+
+    def open_up(t, h):
+        m = mats[3, h, :, :32]
+        for lo in (0, 1):
+            def body(i, _):
+                lanes = pl.ds(pl.multiple_of(i * 640, 128), 640)
+                rows = jnp.concatenate(
+                    [rz[h * 4 + lo, t, :, lanes], rz[h * 4 + 2 + lo, t, :, lanes]], axis=0
+                )
+                to = pl.ds(pl.multiple_of(lo * 1280 + i * 640, 128), 640)
+                s1[h, t, :, to] = dot(m, rows).astype(BF)
+                return 0
+
+            lax.fori_loop(0, 2, body, 0)
+
+    def turn(t, h):
+        m = mats[2, h]
+
+        def body(i, _):
+            lanes = pl.ds(pl.multiple_of(i * 512, 512), 512)
+            s2[h, t, :, lanes] = dot(m, r1[h, t, :, lanes]).astype(BF)
+            return 0
+
+        lax.fori_loop(0, 5, body, 0)
+
+    def close(t, h):
+        for hh in (0, 1):
+            m = mats[hh, h]
+
+            def body(i, _):
+                o = dot(m, r2[h, t, :, pl.ds(pl.multiple_of(i * 640, 128), 640)]).astype(BF)
+                c = h * 4 + hh * 2 + i // 2
+                lanes = pl.ds(pl.multiple_of((i % 2) * 640, 128), 640)
+                own[t, c, :, lanes] = o[:32]
+                snd[t, c, :, lanes] = o[32:]
+                return 0
+
+            lax.fori_loop(0, 4, body, 0)
+
+    def step1(t):
+        for i in range(1, N_KV):
+            c = (kv - i + N_KV) % N_KV
+            remote(
+                d.at[3 * c + t], rz.at[c, t], z_s.at[t, i - 1], z_r.at[t, i - 1], place.head(i)
+            ).wait_recv()
+        for h in (0, 1):
+            open_up(t, h)
+            sent.extend(
+                axis_send(place, 1 - h, s1.at[h, t], r1.at[h, t], p1_s.at[h, t], p1_r.at[h, t])
+            )
+
+    def step2(t):
+        for h in (0, 1):
+            axis_wait(place, 1 - h, s1.at[h, t], r1.at[h, t], p1_s.at[h, t], p1_r.at[h, t])
+            turn(t, h)
+            sent.extend(axis_send(place, h, s2.at[h, t], r2.at[h, t], p2_s.at[h, t], p2_r.at[h, t]))
+
+    last = []
+
+    def step3(t):
+        for h in (0, 1):
+            axis_wait(place, h, s2.at[h, t], r2.at[h, t], p2_s.at[h, t], p2_r.at[h, t])
+            close(t, h)
+            part = pl.ds(4 * h, 4)
+            cp = remote(
+                snd.at[t, part], rcv.at[t, part], core_s.at[t, h], core_r.at[t, h], place.core()
+            )
+            cp.start()
+            sent.append(cp)
+            last.append(cp)
+
+    def step4(t):
+        last[2 * t].wait_recv()
+        last[2 * t + 1].wait_recv()
+
+        def body(c, _):
+            wide = pl.ds(pl.multiple_of(c * 1024, 1024), 1024)
+            thin = pl.ds(pl.multiple_of(c * 128, 128), 128)
+            gq[t, :, wide] = own[t, c, :, 0:1024] + rcv[t, c, :, 0:1024]
+            gk[t, :, thin] = own[t, c, :, 1024:1152] + rcv[t, c, :, 1024:1152]
+            gv[t, :, thin] = own[t, c, :, 1152:1280] + rcv[t, c, :, 1152:1280]
+            return 0
+
+        lax.fori_loop(0, N_KV, body, 0)
+
+    step1(0)
+    step1(1)
+    step2(0)
+    step2(1)
+    step3(0)
+    step1(2)
+    step2(2)
+    step3(1)
+    step4(0)
+    step4(1)
+    step3(2)
+    step4(2)
+    for cp in sent:
+        cp.wait_send()
+
+
+def back(d, mats):
+    vm = pl.BlockSpec(memory_space=pltpu.VMEM)
+    sem = pltpu.SemaphoreType.DMA
+    half = pltpu.VMEM((2, 3, 64, 2560), BF)
+    full = pltpu.VMEM((3, N_KV, SLOTS, 1280), BF)
+    return pl.pallas_call(
+        back_kernel,
+        out_shape=[
+            jax.ShapeDtypeStruct((3, SLOTS, 8192), BF),
+            jax.ShapeDtypeStruct((3, SLOTS, 1024), BF),
+            jax.ShapeDtypeStruct((3, SLOTS, 1024), BF),
+        ],
+        in_specs=[vm] * 2,
+        out_specs=[vm] * 3,
+        scratch_shapes=[
+            pltpu.VMEM((N_KV, 3, GROUP, 1280), BF),
+            half, half, half, half,
+            full, full, full,
+            sem((3, 7)), sem((3, 7)),
+            sem((2, 3, 3)), sem((2, 3, 3)),
+            sem((2, 3, 3)), sem((2, 3, 3)),
+            sem((3, 2)), sem((3, 2)),
+        ],
+        compiler_params=pltpu.CompilerParams(
+            collective_id=1, has_side_effects=True, vmem_limit_bytes=VMEM_BYTES
+        ),
+        name="back",
+    )(d, mats)
+
+
+def attend_kernel(
+    lens, plen_ref, qk, gv, keys, values, dall, dkeys, dvalues,
+    qc, gc, cat, qs, gs, kt, sc, dp, scl, dpl, acck, accv, accok, accov, dqt,
+):
+    scale = HD ** -0.5
+    plen = plen_ref[0]
+    ends = []
+    total = jnp.int32(0)
+    for s in range(GROUP):
+        total = total + lens[s]
+        ends.append(total)
+    starts = [jnp.int32(0)] + ends[:-1]
+    chunks = (total + CHUNK - 1) // CHUNK
+    blocks = (plen + KB - 1) // KB
+
+    def rank_of(at):
+        tok, slot = at // GROUP, at % GROUP
+        rank = jnp.full(at.shape, -1, jnp.int32)
+        for s in range(GROUP):
+            rank = jnp.where((slot == s) & (tok < lens[s]), starts[s] + tok, rank)
+        return rank
+
+    def start_of(row):
+        first = jnp.zeros(row.shape, jnp.int32)
+        for s in range(GROUP):
+            first = jnp.where(row >= starts[s], starts[s], first)
+        return first
+
+    rank_row = rank_of(lax.broadcasted_iota(jnp.int32, (1, ROWS), 1))
+    qc[0:CHUNK, :] = jnp.zeros((CHUNK, 1152), BF)
+    gc[0:CHUNK, :] = jnp.zeros((CHUNK, 1152), BF)
+    cat[...] = jnp.zeros((ROWS, 1280), BF)
+    accok[...] = jnp.zeros_like(accok)
+    accov[...] = jnp.zeros_like(accov)
+    acck[...] = jnp.zeros_like(acck)
+    accv[...] = jnp.zeros_like(accv)
+
+    def compact(i, _):
+        at = lax.broadcasted_iota(jnp.int32, (CHUNK, ROWS), 0) + i * CHUNK
+        pick = jnp.where(at == rank_row, 1.0, 0.0).astype(BF)
+        to = pl.ds(pl.multiple_of(i * CHUNK + CHUNK, CHUNK), CHUNK)
+        for lo in range(0, 1152, 384):
+            qc[to, lo : lo + 384] = dot(pick, qk[:, lo : lo + 384]).astype(BF)
+            gc[to, lo : lo + 384] = dot(pick, gv[:, lo : lo + 384]).astype(BF)
+        return 0
+
+    lax.fori_loop(0, chunks, compact, 0)
+
+    def turn_keys(b, _):
+        rows = pl.ds(pl.multiple_of(b * KB, KB), KB)
+        kt[b] = jnp.transpose(keys[rows, :].astype(F32)).astype(BF)
+        return 0
+
+    lax.fori_loop(0, blocks, turn_keys, 0)
+
+    def fold_max(s):
+        return jnp.max(s.reshape(s.shape[0] // 8, 8, LANES), axis=0)
+
+    def fold_sum(s):
+        return jnp.sum(s.reshape(s.shape[0] // 8, 8, LANES), axis=0)
+
+    def chunk(i, _):
+        here = pl.ds(pl.multiple_of(i * CHUNK + CHUNK, CHUNK), CHUNK)
+        window = pl.ds(pl.multiple_of(i * CHUNK, CHUNK), WIN)
+        for h in range(HG):
+            qs[h * CHUNK : (h + 1) * CHUNK, :] = qc[here, h * HD : (h + 1) * HD]
+            gs[h * CHUNK : (h + 1) * CHUNK, :] = gc[here, h * HD : (h + 1) * HD]
+        q_t = jnp.transpose(qs[...].astype(F32)).astype(BF)
+        g_t = jnp.transpose(gs[...].astype(F32)).astype(BF)
+        own_k = qc[window, 1024:1152]
+        own_v = gc[window, 1024:1152]
+
+        def score(b, m):
+            rows = pl.ds(pl.multiple_of(b * KB, KB), KB)
+            s = dot(keys[rows, :], q_t)
+            seen = lax.broadcasted_iota(jnp.int32, (KB, 1), 0) + b * KB < plen
+            s = jnp.where(seen, s, -jnp.inf)
+            sc[rows, :] = s
+            return jnp.maximum(m, fold_max(s))
+
+        m8 = lax.fori_loop(0, blocks, score, jnp.full((8, LANES), -jnp.inf, F32))
+        row = lax.broadcasted_iota(jnp.int32, (1, LANES), 1) % CHUNK + i * CHUNK
+        first = start_of(row)
+        key = lax.broadcasted_iota(jnp.int32, (WIN, 1), 0) + (i - 1) * CHUNK
+        s = jnp.where((key <= row) & (key >= first), dot(own_k, q_t), -jnp.inf)
+        scl[...] = s
+        m = jnp.max(jnp.maximum(m8, fold_max(s)), axis=0, keepdims=True)
+        shift = m * (scale * LOG2E)
+
+        def weigh(s, v):
+            e = jnp.exp2(s * (scale * LOG2E) - shift)
+            dpv = dot(v, g_t)
+            return e, dpv
+
+        def soft(b, carry):
+            l, dl = carry
+            rows = pl.ds(pl.multiple_of(b * KB, KB), KB)
+            e, dpv = weigh(sc[rows, :], values[rows, :])
+            sc[rows, :] = e
+            dp[rows, :] = dpv
+            return l + fold_sum(e), dl + fold_sum(e * dpv)
+
+        zero = jnp.zeros((8, LANES), F32)
+        l8, d8 = lax.fori_loop(0, blocks, soft, (zero, zero))
+        e, dpv = weigh(scl[...], own_v)
+        scl[...] = e
+        dpl[...] = dpv
+        l = jnp.sum(l8 + fold_sum(e), axis=0, keepdims=True)
+        inv = 1.0 / l
+        delta = jnp.sum(d8 + fold_sum(e * dpv), axis=0, keepdims=True) * inv
+        dqt[...] = jnp.zeros_like(dqt)
+
+        def grads(e, dpv):
+            p = e * inv
+            ds = p * (dpv - delta)
+            return p.astype(BF), ds.astype(BF)
+
+        def grad(b, _):
+            rows = pl.ds(pl.multiple_of(b * KB, KB), KB)
+            p, ds = grads(sc[rows, :], dp[rows, :])
+            accv[rows, :] += dot(p, gs[...])
+            acck[rows, :] += dot(ds, qs[...])
+            dqt[...] += dot(kt[b], ds)
+            return 0
+
+        lax.fori_loop(0, blocks, grad, 0)
+        p, ds = grads(scl[...], dpl[...])
+        accov[window, :] += dot(p, gs[...])
+        accok[window, :] += dot(ds, qs[...])
+        k_t = jnp.transpose(own_k.astype(F32)).astype(BF)
+        dq = jnp.transpose((dqt[...] + dot(k_t, ds)) * scale).astype(BF)
+        out = pl.ds(pl.multiple_of(i * CHUNK, CHUNK), CHUNK)
+        for h in range(HG):
+            cat[out, h * HD : (h + 1) * HD] = dq[h * CHUNK : (h + 1) * CHUNK, :]
+        return 0
+
+    lax.fori_loop(0, chunks, chunk, 0)
+
+    def close(b, _):
+        rows = pl.ds(pl.multiple_of(b * KB, KB), KB)
+        dkeys[rows, :] = (acck[rows, :] * scale).astype(BF)
+        dvalues[rows, :] = accv[rows, :].astype(BF)
+        return 0
+
+    lax.fori_loop(0, PLEN // KB, close, 0)
+    cat[:, 1024:1152] = (accok[CHUNK:, :] * scale).astype(BF)
+    cat[:, 1152:1280] = accov[CHUNK:, :].astype(BF)
+
+    def spread(b, _):
+        rows = pl.ds(pl.multiple_of(b * 128, 128), 128)
+        rank = rank_of(lax.broadcasted_iota(jnp.int32, (128, 1), 0) + b * 128)
+        at = lax.broadcasted_iota(jnp.int32, (128, ROWS), 1)
+        pick = jnp.where(at == rank, 1.0, 0.0).astype(BF)
+        for lo in range(0, 1280, 256):
+            dall[rows, lo : lo + 256] = dot(pick, cat[:, lo : lo + 256]).astype(BF)
+        return 0
+
+    lax.fori_loop(0, ROWS // 128, spread, 0)
+
+
+def attend(lens, plen, qk, gv, keys, values):
+    vm = pl.BlockSpec(memory_space=pltpu.VMEM)
+    sm = pl.BlockSpec(memory_space=pltpu.SMEM)
+    return pl.pallas_call(
+        attend_kernel,
+        out_shape=[
+            jax.ShapeDtypeStruct((ROWS, 1280), BF),
+            jax.ShapeDtypeStruct((PLEN, HD), BF),
+            jax.ShapeDtypeStruct((PLEN, HD), BF),
+        ],
+        in_specs=[sm, sm, vm, vm, vm, vm],
+        out_specs=[vm] * 3,
+        scratch_shapes=[
+            pltpu.VMEM((ROWS + CHUNK, 1152), BF),
+            pltpu.VMEM((ROWS + CHUNK, 1152), BF),
+            pltpu.VMEM((ROWS, 1280), BF),
+            pltpu.VMEM((LANES, HD), BF),
+            pltpu.VMEM((LANES, HD), BF),
+            pltpu.VMEM((PLEN // KB, HD, KB), BF),
+            pltpu.VMEM((PLEN, LANES), F32),
+            pltpu.VMEM((PLEN, LANES), F32),
+            pltpu.VMEM((WIN, LANES), F32),
+            pltpu.VMEM((WIN, LANES), F32),
+            pltpu.VMEM((PLEN, HD), F32),
+            pltpu.VMEM((PLEN, HD), F32),
+            pltpu.VMEM((ROWS + CHUNK, HD), F32),
+            pltpu.VMEM((ROWS + CHUNK, HD), F32),
+            pltpu.VMEM((HD, LANES), F32),
+        ],
+        compiler_params=pltpu.CompilerParams(vmem_limit_bytes=VMEM_BYTES),
+        name="attend",
+    )(lens, plen, qk, gv, keys, values)
+
+
+def fast(q, g, k, v, keys, values, mats, mats_back, lens, plen):
+    qk, gv = there(*(jnp.transpose(a, (1, 0, 2)) for a in (q, g, k, v)), mats)
+    d, dkeys, dvalues = attend(
+        lens, plen, qk.reshape(ROWS, 1152), gv.reshape(ROWS, 1152), keys, values
+    )
+    gq, gk, gvv = back(d.reshape(RT, GROUP, 1280), mats_back)
+    return (*(jnp.transpose(a, (1, 0, 2)) for a in (gq, gk, gvv)), dkeys, dvalues)
+
+
+def per_device(
+    q_tokens, grad_tokens, roll_keys, roll_values, prompt_keys, prompt_values,
+    slot_prompt, prompt_owner, roll_len, prompt_len,
+):
+    me = lax.axis_index("roll")
+    fits, mats, mats_back, lens, plen = route_tables(
+        slot_prompt, prompt_owner, roll_len, prompt_len, me
+    )
+    arrays = (q_tokens, grad_tokens, roll_keys, roll_values, prompt_keys, prompt_values)
+    return lax.cond(
+        fits,
+        lambda: fast(*arrays, mats, mats_back, lens, plen),
+        lambda: general(*arrays, slot_prompt, prompt_owner, roll_len, prompt_len),
+    )
+
+
 def solution(mesh):
     in_specs = (
         P("roll", "kv", None),

time: 758 us -> 187 us (0.25); the launches traced: 749 us -> 187 us
  local copies, waits for them, and re-layouts: 203 us -> 3.68 us
  waiting for transfers between devices: 178 us -> 0 us
  Pallas kernels: 0 us -> 169 us
  matrix products: 155 us -> 0 us
  other arithmetic: 101 us -> 12.3 us
  starting transfers between devices: 67.3 us -> 0 us
  blocking collectives: 42.8 us -> 0 us
    all_to_all x13 -> x0, waiting for transfers between devices: 178 us -> none  [the longest x1 39.2 us: per_device(): lax.all_to_all(q_back, 'roll', split_axis=0, concat_axis=0, tiled=True)]
    pallas_call x0 -> x3, Pallas kernels: none -> 169 us  [the longest x1 81.4 us: there(): pl.pallas_call(there_kernel, out_shape=[jax.ShapeDtypeStruct((RT, GROUP,...]
    dot_general x80 -> x0, matrix products: 155 us -> none  [the longest x8 33.4 us: step(): jnp.einsum('ntkjd,pkd->ntkjp', grads_b, pvalues, preferred_element_type=f32)]
    all_to_all x13 -> x0, starting transfers between devices: 67.3 us -> none  [the longest x1 9.79 us: per_device(): lax.all_to_all(sent_k, 'roll', split_axis=0, concat_axis=0, tiled=True)]
    unnamed x36 -> x15, local copies, waits for them, and re-layouts: 61.5 us -> 3.09 us
    all_to_all x1 -> x0, blocking collectives: 42.8 us -> none  [per_device(): lax.all_to_all(sent_q, 'roll', split_axis=0, concat_axis=0, tiled=True)]
    another operation x21 -> x5, other arithmetic: 37.9 us -> 0.1 us  [the longest x2 0.08 us: route_tables(): there = jnp.stack([first, second, third])]
    all_to_all x11 -> x0, local copies, waits for them, and re-layouts: 34.3 us -> none  [the longest x2 14.1 us: per_device(): lax.all_to_all(q_tokens, 'kv', split_axis=2, concat_axis=1, tiled=True)]
  transfers between devices with their start and end apart: 13 -> 0, of which waited for: 11 -> 0; matrix products, arithmetic and copies ran while one was open for 19% -> 0% of each run, Pallas kernels for 0% -> 0%
where the time goes in v1:
time: 187 us
  Pallas kernels  169 us (90%)
  other arithmetic  12.3 us (7%)
  local copies, waits for them, and re-layouts  3.68 us (2%)
    pallas_call x1, Pallas kernels, there(): pl.pallas_call(there_kernel, out_shape=[jax.ShapeDtypeStruct((RT, GROUP,...  81.4 us
    pallas_call x1, Pallas kernels, back(): pl.pallas_call(back_kernel, out_shape=[jax.ShapeDtypeStruct((3, SLOTS, 81...  55.3 us
    pallas_call x1, Pallas kernels, attend(): pl.pallas_call(attend_kernel, out_shape=[jax.ShapeDtypeStruct((ROWS, 1280...  32.4 us
    reduce_sum x1, other arithmetic, route_tables(): rank = jnp.sum(same.astype(jnp.int32), axis=2)  4.19 us

profile of v1, /device:TPU:1, one launch (start us, length us, event | category | flops | bytes accessed | tf_op | source)
XLA Modules:
  0.0 186.8 jit_solution(10962008413840281449)
XLA Ops:
  0.6 0.0 copy-start.21
  0.7 0.8 broadcast_add_fusion.4
  1.5 1.0 select_reduce_fusion.6
  2.5 0.7 fusion.95
  3.2 0.1 multiply_add_fusion.2
  3.4 0.3 iota_compare_fusion.7
  3.7 4.2 %convert_reduce_fusion.2 = s32[5,1024]{1,0:T(8,128)S(1)} fusion(s32[5,1024]{1,0:T(8,128)S(1)} %broadcast_select_fusion.3, pred[1024,1024]{1,0:T(8,128)(4,1)S(1)} %iota_compare_fusion.7), kind=kLoop, calls=%fused_computation.159 | loop fusion | flops 20966400 | bytes 1089536 | tf_op jit(solution)/shard_map/reduce_sum | solution.py:287
  7.9 0.1 constant_dynamic-slice_fusion.1
  8.0 0.1 add_select_fusion.20
  8.1 0.1 add_select_fusion.19
  8.3 0.7 broadcast_add_fusion.2
  9.1 0.2 select_reduce_fusion.5
  9.3 0.6 copy-done.22
  9.9 0.1 reshape.1363
  10.0 0.1 stack_reshape.11
  10.1 0.1 stack_reshape.12
  10.2 0.1 stack_reshape.13
  10.3 0.8 fusion.62
  11.1 0.1 add_bitcast_fusion.1
  11.2 0.7 fusion.63
  11.8 0.6 fusion.64
  13.2 171.1 %conditional.1 = (bf16[32,3,8192]{2,0,1:T(8,128)(2,1)S(1)}, bf16[32,3,1024]{2,0,1:T(8,128)(2,1)S(1)}, bf16[32,3,1024]{2,0,1:T(8,128)(2,1)S(1)}, bf16[2048,128]{1,0:T(8,128)(2,1)}, bf16[2048,128]{1,0:T(8,128)(2,1)}) conditional(s32[]{:T(128)} %convert_element_type.65, (s32[1024]{0:T(1024)S(1)}, s32[32]{0:T(128)S(1)}, ...), branch_computations={%region_5.33_spmd, %region_28.34_spmd} | conditional | flops 1047797248 | bytes 216535104 | solution.py:914
  13.4 0.0 copy-start.30
  13.4 0.0 copy-start.17
  13.5 81.4 %there.1 = (bf16[24,16,1152]{2,1,0:T(8,128)(2,1)}, bf16[24,16,1152]{2,1,0:T(8,128)(2,1)}) custom-call(bf16[3,32,8192]{2,1,0:T(8,128)(2,1)S(1)} %bitcast.426, bf16[3,32,8192]{2,1,0:T(8,128)(2,1)S(1)} %bitcast.427, bf16[3,32,1024]{2,1,0:T(8,128)(2,1)S(1)} %bitcast.444, bf16[3,32,1024]{2,1,0:T(8,128)(2,1)} %bitcast.445, ...), custom_call_target="tpu_custom_call" | custom-call | tf_op jit(solution)/shard_map/cond/branch_1_fun/there/pallas_call | solution.py:528
  94.9 0.6 fusion.4
  95.5 1.2 fusion.5.lens
  96.7 32.4 %attend.1 = (bf16[384,1280]{1,0:T(8,128)(2,1)}, bf16[2048,128]{1,0:T(8,128)(2,1)}, bf16[2048,128]{1,0:T(8,128)(2,1)}) custom-call(s32[16]{0:T(128)} %fusion.5.lens, s32[1]{0:T(128)} %bitcast.40.plen_ref, bf16[384,1152]{1,0:T(8,128)(2,1)} %bitcast.442, bf16[384,1152]{1,0:T(8,128)(2,1)} %bitcast.443, bf16[2048,128]{1,0:T(8,128)(2,1)} %get-tuple-element.143.keys, ...), custom_call_target="tpu_custom_call" | custom-call | tf_op jit(solution)/shard_map/cond/branch_1_fun/attend/pallas_call | solution.py:865
  129.0 55.3 %back.1 = (bf16[3,32,8192]{2,1,0:T(8,128)(2,1)S(1)}, bf16[3,32,1024]{2,1,0:T(8,128)(2,1)S(1)}, bf16[3,32,1024]{2,1,0:T(8,128)(2,1)S(1)}) custom-call(bf16[24,16,1280]{2,1,0:T(8,128)(2,1)} %bitcast.441, bf16[4,2,64,64]{3,2,1,0:T(8,128)(2,1)S(1)} %copy-done.18), custom_call_target="tpu_custom_call" | custom-call | tf_op jit(solution)/shard_map/cond/branch_1_fun/back/pallas_call | solution.py:677
  184.3 1.1 copy.390
  185.5 0.7 copy.391
  186.2 0.7 copy.392
  (36 shorter events, 0.4 us)
Async XLA Ops:
  0.6 12.5 %copy-start.26 = (s32[32]{0:T(128)S(1)}, s32[32]{0:T(128)}, u32[]{:S(2)}) copy-start(s32[32]{0:T(128)} %param.31) | copy-start | bytes 388
  0.6 12.5 %copy-start.21 = (s32[1024]{0:T(1024)S(1)}, s32[1024]{0:T(1024)}, u32[]{:S(2)}) copy-start(s32[1024]{0:T(1024)} %param.30) | copy-start | bytes 12292
  0.7 12.5 %copy-start.5 = (bf16[32,3,8192]{2,0,1:T(8,128)(2,1)S(1)}, bf16[32,3,8192]{2,0,1:T(8,128)(2,1)}, u32[]{:S(2)}) copy-start(bf16[32,3,8192]{2,0,1:T(8,128)(2,1)} %param.24) | copy-start | bytes 4718596
  0.7 12.5 %copy-start.6 = (bf16[32,3,8192]{2,0,1:T(8,128)(2,1)S(1)}, bf16[32,3,8192]{2,0,1:T(8,128)(2,1)}, u32[]{:S(2)}) copy-start(bf16[32,3,8192]{2,0,1:T(8,128)(2,1)} %param.25) | copy-start | bytes 4718596
  0.7 12.5 %copy-start.15 = (bf16[32,3,1024]{2,0,1:T(8,128)(2,1)S(1)}, bf16[32,3,1024]{2,0,1:T(8,128)(2,1)}, u32[]{:S(2)}) copy-start(bf16[32,3,1024]{2,0,1:T(8,128)(2,1)} %param.26) | copy-start | bytes 589828
  9.3 0.6 copy-start.22
  13.4 81.4 %copy-start.30 = (s32[32]{0:T(128)S(1)}, s32[32]{0:T(128)}, u32[]{:S(2)}) copy-start(s32[32]{0:T(128)} %get-tuple-element.171) | copy-start | bytes 388 | tf_op jit(solution)/shard_map/cond
  13.4 83.3 %copy-start.17 = (bf16[2048,128]{1,0:T(8,128)(2,1)S(1)}, bf16[2048,128]{1,0:T(8,128)(2,1)}, u32[]{:S(2)}) copy-start(bf16[2048,128]{1,0:T(8,128)(2,1)} %get-tuple-element.144.values) | copy-start | bytes 1572868 | tf_op jit(solution)/shard_map/cond
  13.5 115.6 %copy-start.18 = (bf16[4,2,64,64]{3,2,1,0:T(8,128)(2,1)S(1)}, bf16[4,2,64,64]{3,2,1,0:T(8,128)(2,1)}, u32[]{:S(2)}) copy-start(bf16[4,2,64,64]{3,2,1,0:T(8,128)(2,1)} %get-tuple-element.146.mats) | copy-start | bytes 196612 | tf_op jit(solution)/shard_map/cond

commit v2 on v0

--- a/solution.py
+++ b/solution.py
@@ -1,6 +1,8 @@
 import jax
 import jax.numpy as jnp
 from jax import lax
+from jax.experimental import pallas as pl
+from jax.experimental.pallas import tpu as pltpu
 from jax.sharding import PartitionSpec as P
 
 HD = 128
@@ -171,7 +173,7 @@
     )
 
 
-def per_device(
+def general(
     q_tokens,
     grad_tokens,
     roll_keys,
@@ -236,6 +238,649 @@
     return (grad_query, grad_okeys, grad_ovalues, grad_pkeys, grad_pvalues)
 
 
+CAP = 8
+N_KV = 8
+N_ROLL = 32
+SLOTS = 32
+TSLOTS = 1024
+RT = 24
+PLEN = 2048
+HG = 8
+MESH = pl.DeviceIdType.MESH
+BF = jnp.bfloat16
+F32 = jnp.float32
+LANES = 8 * N_KV * HG
+KB = 512
+OWN = 3 * 8 * N_KV
+LOG2E = 1.4426950408889634
+VMEM_BYTES = 62 * 1024 * 1024
+
+
+def dot(a, b):
+    return jnp.dot(a, b, preferred_element_type=F32)
+
+
+def dot_t(a, b):
+    return lax.dot_general(a, b, (((1,), (1,)), ((), ())), preferred_element_type=F32)
+
+
+def tables_kernel(where, owner, prompt_len, slots, lens, mats, mats_back, info):
+    me, kv = where[0], where[1]
+    x, y, c = me // 8, (me // 2) % 4, me % 2
+    row = (1, TSLOTS)
+    n = lax.broadcasted_iota(jnp.int32, row, 1)
+    prompt = slots[...]
+    live = prompt >= 0
+    dest = jnp.zeros(row, jnp.int32)
+    plen = jnp.int32(0)
+    for p in range(N_ROLL):
+        dest = jnp.where(prompt == p, owner[p], dest)
+        plen = plen + jnp.where(owner[p] == me, prompt_len[p], 0)
+    src = n // SLOTS
+    xs, ys, cs = src // 8, (src // 2) % 4, src % 2
+    xd, yd, cd = dest // 8, (dest // 2) % 4, dest % 2
+    chip = xs * 4 + ys
+    before = (
+        lax.broadcasted_iota(jnp.int32, (128, 128), 0) < lax.broadcasted_iota(jnp.int32, (128, 128), 1)
+    )
+    both = jnp.concatenate(
+        [jnp.where(before, 1.0, 0.0), jnp.ones((128, 128), F32)], axis=1
+    ).astype(BF)
+
+    def marks(at, count):
+        rows = lax.broadcasted_iota(jnp.int32, (count, TSLOTS), 0)
+        return jnp.where(rows == at, 1.0, 0.0)
+
+    def rank_in(key, count):
+        mark = marks(jnp.where(live, key, -1), count)
+        total = jnp.zeros((count, 128), F32)
+        parts = []
+        for b in range(TSLOTS // 128):
+            m = mark[:, b * 128 : (b + 1) * 128]
+            o = dot(m.astype(BF), both)
+            parts.append(jnp.sum(m * (o[:, :128] + total), axis=0, keepdims=True))
+            total = total + o[:, 128:]
+        return jnp.concatenate(parts, axis=1).astype(jnp.int32)
+
+    first = (rank_in((chip * 2 + cd) * 4 + xd, 128), rank_in((chip * 2 + cd) * 4 + yd, 128))
+    second = (
+        rank_in(((xd * 4 + ys) * 2 + cd) * 4 + yd, 128),
+        rank_in(((xs * 4 + yd) * 2 + cd) * 4 + xd, 128),
+    )
+    last = rank_in(dest, N_ROLL)
+    most = jnp.maximum(jnp.maximum(first[0], first[1]), jnp.maximum(second[0], second[1]))
+    info[0] = jnp.where(jnp.max(most) < CAP, 1, 0)
+    info[1] = plen
+
+    mine = live & (dest == me)
+    near = live & (cd == c) & (chip == x * 4 + y)
+    seat = n % SLOTS + jnp.where(cs == c, 0, SLOTS)
+    seat = marks(jnp.where(near, seat, -1), 64).astype(BF)
+    for h in (0, 1):
+        s1, s2 = (xs, ys) if h == 0 else (ys, xs)
+        d1, d2 = (xd, yd) if h == 0 else (yd, xd)
+        mid = live & (cd == c) & ((ys == y) & (xd == x) if h == 0 else (xs == x) & (yd == y))
+
+        def wide(place, rank, ok, part):
+            return marks(jnp.where(ok, (place * 2 + part) * CAP + rank, -1), 64).astype(BF)
+
+        mats[h, 0] = dot_t(marks(jnp.where(near, d1 * CAP + first[h], -1), 64).astype(BF), seat).astype(BF)
+        turn = jnp.zeros((64, 64), F32)
+        turn_back = jnp.zeros((64, 64), F32)
+        ends = [jnp.zeros((64, 64), F32)] * 3
+        end_back = jnp.zeros((64, 64), F32)
+        for part in (0, 1):
+            mats_back[h, part] = dot_t(seat, wide(d1, first[h], near, part)).astype(BF)
+            a, b = wide(s1, first[h], mid, part), wide(d2, second[h], mid, part)
+            turn = turn + dot_t(b, a)
+            turn_back = turn_back + dot_t(a, b)
+            a = wide(s2, second[h], mine, part)
+            b = marks(jnp.where(mine, part * GROUP + last, -1), 64).astype(BF)
+            end_back = end_back + dot_t(a, b)
+            for t in range(3):
+                if h == 0:
+                    ends[t] = ends[t] + dot_t(b, a)
+                else:
+                    valid = mine & (3 * kv + t < lens[...])
+                    b = marks(jnp.where(valid, part * GROUP + last, -1), 64).astype(BF)
+                    ends[t] = ends[t] + dot_t(b, a)
+        mats[h, 1] = turn.astype(BF)
+        for t in range(3):
+            mats[h, 2 + t] = ends[t].astype(BF)
+        mats_back[h, 2] = turn_back.astype(BF)
+        mats_back[h, 3] = end_back.astype(BF)
+
+
+def route_tables(slot_prompt, prompt_owner, roll_len, prompt_len):
+    where = jnp.stack([lax.axis_index("roll"), lax.axis_index("kv")]).astype(jnp.int32)
+    vm = pl.BlockSpec(memory_space=pltpu.VMEM)
+    sm = pl.BlockSpec(memory_space=pltpu.SMEM)
+    return pl.pallas_call(
+        tables_kernel,
+        out_shape=[
+            jax.ShapeDtypeStruct((2, 5, 64, 64), BF),
+            jax.ShapeDtypeStruct((2, 4, 64, 64), BF),
+            jax.ShapeDtypeStruct((2,), jnp.int32),
+        ],
+        in_specs=[sm, sm, sm, vm, vm],
+        out_specs=[vm, vm, sm],
+        compiler_params=pltpu.CompilerParams(vmem_limit_bytes=VMEM_BYTES),
+        name="tables",
+    )(where, prompt_owner, prompt_len, slot_prompt.reshape(1, TSLOTS), roll_len.reshape(1, TSLOTS))
+
+
+class Place:
+    def __init__(self):
+        self.kv = lax.axis_index("kv")
+        self.me = lax.axis_index("roll")
+        self.x = self.me // 8
+        self.y = (self.me // 2) % 4
+        self.c = self.me % 2
+
+    def pos(self, axis):
+        return self.x if axis == 0 else self.y
+
+    def chip(self, axis, step):
+        if axis == 0:
+            return (self.kv, ((self.x + step) % 4) * 8 + self.y * 2 + self.c)
+        return (self.kv, self.x * 8 + ((self.y + step) % 4) * 2 + self.c)
+
+    def core(self):
+        return (self.kv, self.x * 8 + self.y * 2 + 1 - self.c)
+
+    def head(self, step):
+        return ((self.kv + step) % N_KV, self.me)
+
+    def greet(self):
+        peers = [self.core()]
+        peers += [self.chip(axis, i) for axis in (0, 1) for i in (1, 2, 3)]
+        peers += [self.head(i) for i in range(1, N_KV)]
+        barrier = pltpu.get_barrier_semaphore()
+        for peer in peers:
+            pl.semaphore_signal(barrier, inc=1, device_id=peer, device_id_type=MESH)
+        pl.semaphore_wait(barrier, len(peers))
+
+
+def remote(src, dst, send, recv, peer):
+    return pltpu.make_async_remote_copy(
+        src_ref=src, dst_ref=dst, send_sem=send, recv_sem=recv, device_id=peer, device_id_type=MESH
+    )
+
+
+def rows16(p):
+    return pl.ds(pl.multiple_of(p * 16, 16), 16)
+
+
+def axis_copies(place, axis, out, land, send, recv):
+    p = place.pos(axis)
+    return [
+        remote(
+            out.at[rows16((p + i) % 4)], land.at[rows16(p)], send.at[i - 1], recv.at[i - 1],
+            place.chip(axis, i),
+        )
+        for i in (1, 2, 3)
+    ]
+
+
+def axis_send(place, axis, out, land, send, recv):
+    for cp in axis_copies(place, axis, out, land, send, recv):
+        cp.start()
+    mine = rows16(place.pos(axis))
+    land[mine, :] = out[mine, :]
+
+
+def axis_wait(place, axis, out, land, send, recv):
+    p = place.pos(axis)
+    for i in (1, 2, 3):
+        q = rows16((p - i + 4) % 4)
+        remote(
+            out.at[q], land.at[q], send.at[i - 1], recv.at[i - 1], place.chip(axis, i)
+        ).wait_recv()
+
+
+def head_copies(place, out, land, send, recv):
+    return [
+        remote(
+            out.at[(place.kv + i) % N_KV], land.at[place.kv], send.at[i - 1], recv.at[i - 1],
+            place.head(i),
+        )
+        for i in (4, 3, 5, 2, 6, 1, 7)
+    ]
+
+
+def head_send(place, out, land, send, recv):
+    for cp in head_copies(place, out, land, send, recv):
+        cp.start()
+    land[place.kv] = out[place.kv]
+
+
+def head_wait(place, out, land, send, recv):
+    for i in range(1, N_KV):
+        c = (place.kv - i + N_KV) % N_KV
+        remote(
+            out.at[c], land.at[c], send.at[i - 1], recv.at[i - 1], place.head(i)
+        ).wait_recv()
+
+
+def mega_kernel(
+    info, q, g, k, v, mats, mats_back, keys, values,
+    gq, gk, gv, dkeys, dvalues,
+    cq, cg, ck, cv,
+    s1a, s1b, r1a, r1b, s2a, s2b, r2a, r2b, s3a, s3b, za, zb,
+    qs, gs, ko, vo, kt, sc, dp, acck, accv, accok, accov, dqf, da, dl,
+    rza, rzl, b1a, b1l, t1a, t1l, b2a, b2l, t2a, t2l, snda, sndl, rcva, rcvl,
+    core_s, core_r, p1_s, p1_r, p2_s, p2_r, z_s, z_r,
+    y_s, y_r, u1_s, u1_r, u2_s, u2_r, home_s, home_r,
+):
+    place = Place()
+    place.greet()
+    scale = HD ** -0.5
+    plen = info[1]
+
+    def core_copies(t):
+        names = [(q.at[t], cq.at[t], t, 0), (g.at[t], cg.at[t], t, 1)]
+        if t == 0:
+            names += [(k, ck, 3, 0), (v, cv, 3, 1)]
+        return [
+            remote(a, b, core_s.at[i, j], core_r.at[i, j], place.core()) for a, b, i, j in names
+        ]
+
+    def part(first, rest, t, h):
+        return first.at[h] if t == 0 else rest.at[h, t - 1]
+
+    def hop1(t, h):
+        return (place, h, part(s1a, s1b, t, h), part(r1a, r1b, t, h), p1_s.at[h, t], p1_r.at[h, t])
+
+    def hop2(t, h):
+        return (
+            place, 1 - h, part(s2a, s2b, t, h), part(r2a, r2b, t, h), p2_s.at[h, t], p2_r.at[h, t],
+        )
+
+    def hop3(t, h):
+        return (place, part(s3a, s3b, t, h), part(za, zb, t, h), z_s.at[h, t], z_r.at[h, t])
+
+    def pack(t):
+        for cp in core_copies(t):
+            cp.wait_recv()
+        for h in (0, 1):
+            m = mats[h, 0, :32, :]
+            dst = part(s1a, s1b, t, h)
+
+            def put(a, b, tt, lo, hi, at):
+                def one(o):
+                    lanes = pl.ds(o, 512)
+                    rows = jnp.concatenate([a[tt, :, lanes], b[tt, :, lanes]], axis=0)
+                    return dot(m, rows).reshape(4, CAP, 512)
+
+                both = jnp.concatenate([one(lo), one(hi)], axis=1).reshape(64, 512)
+                dst[:, pl.ds(at, 512)] = both.astype(BF)
+
+            big, bigo, small, smallo = (q, cq, k, ck) if h == 0 else (g, cg, v, cv)
+
+            def body(i, _):
+                lo = pl.multiple_of(i * 512, 512)
+                put(big, bigo, t, lo, pl.multiple_of(lo + 4096, 512), lo)
+                return 0
+
+            lax.fori_loop(0, 8, body, 0)
+            if t == 0:
+                for tt in range(3):
+                    put(small, smallo, tt, 0, 512, 4096 + tt * 512)
+
+    def send1(t):
+        for h in (0, 1):
+            axis_send(*hop1(t, h))
+
+    def apply(m, src, dst):
+        def body(i, _):
+            lanes = pl.ds(pl.multiple_of(i * 512, 512), 512)
+            dst[:, lanes] = dot(m, src[:, lanes]).astype(BF)
+            return 0
+
+        lax.fori_loop(0, src.shape[1] // 512, body, 0)
+
+    def turn(t):
+        for h in (0, 1):
+            axis_wait(*hop1(t, h))
+            apply(mats[h, 1], part(r1a, r1b, t, h), part(s2a, s2b, t, h))
+            axis_send(*hop2(t, h))
+
+    def finish(t):
+        for h in (0, 1):
+            axis_wait(*hop2(t, h))
+            m = mats[h, 2 + t, :32, :]
+            src, dst = part(r2a, r2b, t, h), part(s3a, s3b, t, h)
+
+            def body(i, _):
+                o = dot(m, src[:, pl.ds(pl.multiple_of(i * 1024, 1024), 1024)]).astype(BF)
+                dst[i, :, 0:1024] = o[:16]
+                dst[i + 4, :, 0:1024] = o[16:]
+                return 0
+
+            lax.fori_loop(0, 4, body, 0)
+            if t == 0:
+                for tt in range(3):
+                    lo = 4096 + tt * 512
+                    at = 1024 + tt * HD
+                    o = dot(mats[h, 2 + tt, :32, :], src[:, lo : lo + 512]).astype(BF)
+                    for i in range(4):
+                        dst[i, :, at : at + HD] = o[:16, i * HD : (i + 1) * HD]
+                        dst[i + 4, :, at : at + HD] = o[16:, i * HD : (i + 1) * HD]
+            head_send(*hop3(t, h))
+
+    def split(block):
+        b = block.astype(F32).reshape(N_KV, 2, 8, HD)
+        return b[:, 0].reshape(64, HD).astype(BF), b[:, 1].reshape(64, HD).astype(BF)
+
+    def prepare(t):
+        for h in (0, 1):
+            head_wait(*hop3(t, h))
+            src, dst = part(za, zb, t, h), (qs, gs)[h]
+            for j in range(HG):
+                a, b = split(src[:, :, j * HD : (j + 1) * HD])
+                dst[0, j * 64 : (j + 1) * 64, :] = a
+                dst[1, j * 64 : (j + 1) * 64, :] = b
+            if t == 0:
+                dst = (ko, vo)[h]
+                for tt in range(3):
+                    at = 1024 + tt * HD
+                    a, b = split(src[:, :, at : at + HD])
+                    dst[0, tt * 64 : (tt + 1) * 64, :] = a
+                    dst[1, tt * 64 : (tt + 1) * 64, :] = b
+
+    def fold_max(s):
+        return jnp.max(s.reshape(s.shape[0] // 8, 8, LANES), axis=0)
+
+    def fold_sum(s):
+        return jnp.sum(s.reshape(s.shape[0] // 8, 8, LANES), axis=0)
+
+    blocks = [slice(b * KB, (b + 1) * KB) for b in range(PLEN // KB)]
+    tail = slice(PLEN, PLEN + OWN)
+
+    def chunk(t, e):
+        q_t = jnp.transpose(qs[e].astype(F32)).astype(BF)
+        g_t = jnp.transpose(gs[e].astype(F32)).astype(BF)
+        m8 = jnp.full((8, LANES), -jnp.inf, F32)
+        for b, rows in enumerate(blocks):
+            s = dot(keys[rows, :], q_t)
+            seen = lax.broadcasted_iota(jnp.int32, (KB, 1), 0) + b * KB < plen
+            s = jnp.where(seen, s, -jnp.inf)
+            sc[rows, :] = s
+            m8 = jnp.maximum(m8, fold_max(s))
+        key = lax.broadcasted_iota(jnp.int32, (OWN, 1), 0)
+        lane = lax.broadcasted_iota(jnp.int32, (1, LANES), 1)
+        key_token = 3 * ((key % 64) // 8) + key // 64
+        row_token = 3 * ((lane % 64) // 8) + t
+        same = (key % 8 == lane % 8) & (key_token <= row_token)
+        s = jnp.where(same, dot(ko[e], q_t), -jnp.inf)
+        sc[tail, :] = s
+        m8 = jnp.maximum(m8, fold_max(s))
+        shift = jnp.max(m8, axis=0, keepdims=True) * (scale * LOG2E)
+
+        l8 = jnp.zeros((8, LANES), F32)
+        d8 = jnp.zeros((8, LANES), F32)
+        for rows in blocks + [tail]:
+            w = jnp.exp2(sc[rows, :] * (scale * LOG2E) - shift)
+            d = dot(vo[e] if rows is tail else values[rows, :], g_t)
+            sc[rows, :] = w
+            dp[rows, :] = d
+            l8 = l8 + fold_sum(w)
+            d8 = d8 + fold_sum(w * d)
+        inv = 1.0 / jnp.sum(l8, axis=0, keepdims=True)
+        delta = jnp.sum(d8, axis=0, keepdims=True) * inv
+
+        dq = jnp.zeros((HD, LANES), F32)
+        for b, rows in enumerate(blocks + [tail]):
+            p = sc[rows, :] * inv
+            ds = (p * (dp[rows, :] - delta)).astype(BF)
+            p = p.astype(BF)
+            if rows is tail:
+                accov[e] += dot(p, gs[e])
+                accok[e] += dot(ds, qs[e])
+                k_t = jnp.transpose(ko[e].astype(F32)).astype(BF)
+            else:
+                accv[rows, :] += dot(p, gs[e])
+                acck[rows, :] += dot(ds, qs[e])
+                k_t = kt[b]
+            dq = dq + dot(k_t, ds)
+        dqf[e] = jnp.transpose(dq * scale)
+
+    def joined(pair):
+        a, b = (p.reshape(N_KV, 8, HD) for p in pair)
+        return jnp.concatenate([a, b], axis=1).astype(BF)
+
+    def piece(rest, final, t, *at):
+        return final.at[at] if t == 2 else rest.at[(t, *at)]
+
+    def back0(t):
+        return (
+            place, dl if t == 2 else da.at[t], rzl if t == 2 else rza.at[t], y_s.at[t], y_r.at[t],
+        )
+
+    def back1(t, h):
+        return (
+            place, 1 - h, piece(b1a, b1l, t, h), piece(t1a, t1l, t, h), u1_s.at[h, t], u1_r.at[h, t],
+        )
+
+    def back2(t, h):
+        return (
+            place, h, piece(b2a, b2l, t, h), piece(t2a, t2l, t, h), u2_s.at[h, t], u2_r.at[h, t],
+        )
+
+    def home(t, h):
+        heads = pl.ds(4 * h, 4)
+        return remote(
+            piece(snda, sndl, t, heads), piece(rcva, rcvl, t, heads),
+            home_s.at[t, h], home_r.at[t, h], place.core(),
+        )
+
+    def leave(t):
+        dst = dl if t == 2 else da.at[t]
+        for j in range(HG):
+            rows = slice(j * 64, (j + 1) * 64)
+            dst[:, :, j * HD : (j + 1) * HD] = joined((dqf[0, rows, :], dqf[1, rows, :]))
+        if t == 2:
+            for tt in range(3):
+                rows = slice(tt * 64, (tt + 1) * 64)
+                at = 1024 + tt * HD
+                dst[:, :, at : at + HD] = joined((accok[0, rows, :] * scale, accok[1, rows, :] * scale))
+                dst[:, :, at + 384 : at + 384 + HD] = joined((accov[0, rows, :], accov[1, rows, :]))
+        head_send(*back0(t))
+
+    def open_up(t):
+        head_wait(*back0(t))
+        src = rzl if t == 2 else rza.at[t]
+        wide, step = (1792, 896) if t == 2 else (1024, 512)
+        for h in (0, 1):
+            m = mats_back[h, 3, :, :32]
+            dst = piece(b1a, b1l, t, h)
+            for lo in (0, 1):
+                for o in range(0, wide, step):
+                    rows = jnp.concatenate(
+                        [src[h * 4 + lo, :, o : o + step], src[h * 4 + 2 + lo, :, o : o + step]], axis=0
+                    )
+                    dst[:, lo * wide + o : lo * wide + o + step] = dot(m, rows).astype(BF)
+            axis_send(*back1(t, h))
+
+    def turn_back(t):
+        for h in (0, 1):
+            axis_wait(*back1(t, h))
+            apply(mats_back[h, 2], piece(t1a, t1l, t, h), piece(b2a, b2l, t, h))
+            axis_send(*back2(t, h))
+
+    def close(t):
+        wide = 1792 if t == 2 else 1024
+        for h in (0, 1):
+            axis_wait(*back2(t, h))
+            src = piece(t2a, t2l, t, h)
+            for hh in (0, 1):
+                m = mats_back[h, hh]
+                for lo in (0, 1):
+                    c = h * 4 + hh * 2 + lo
+                    snd = piece(snda, sndl, t, c)
+                    for o in (0, 512):
+                        r = dot(m, src[:, lo * wide + o : lo * wide + o + 512]).astype(BF)
+                        gq[t, :, c * 1024 + o : c * 1024 + o + 512] = r[:32]
+                        snd[:, o : o + 512] = r[32:]
+                    if t == 2:
+                        r = dot(m, src[:, lo * wide + 1024 : (lo + 1) * wide]).astype(BF)
+                        snd[:, 1024:1792] = r[32:]
+                        for tt in range(3):
+                            lanes = slice(c * HD, (c + 1) * HD)
+                            gk[tt, :, lanes] = r[:32, tt * HD : (tt + 1) * HD]
+                            gv[tt, :, lanes] = r[:32, 384 + tt * HD : 384 + (tt + 1) * HD]
+            home(t, h).start()
+
+    def settle(t):
+        for h in (0, 1):
+            home(t, h).wait_recv()
+        src = rcvl if t == 2 else rcva.at[t]
+        for c in range(N_KV):
+            lanes = slice(c * 1024, (c + 1) * 1024)
+            gq[t, :, lanes] = gq[t, :, lanes] + src[c, :, 0:1024]
+            if t == 2:
+                lanes = slice(c * HD, (c + 1) * HD)
+                for tt in range(3):
+                    at = 1024 + tt * HD
+                    gk[tt, :, lanes] = gk[tt, :, lanes] + src[c, :, at : at + HD]
+                    gv[tt, :, lanes] = gv[tt, :, lanes] + src[c, :, at + 384 : at + 384 + HD]
+
+    for t in range(3):
+        for cp in core_copies(t):
+            cp.start()
+    pack(0)
+    send1(0)
+    pack(1)
+    turn(0)
+    send1(1)
+    pack(2)
+    finish(0)
+    turn(1)
+    send1(2)
+    for b, rows in enumerate(blocks):
+        kt[b] = jnp.transpose(keys[rows, :].astype(F32)).astype(BF)
+    for ref in (acck, accv, accok, accov):
+        ref[...] = jnp.zeros_like(ref)
+    finish(1)
+    prepare(0)
+
+    def body(i, _):
+        chunk(i // 2, i % 2)
+
+        @pl.when(i == 0)
+        def _():
+            turn(2)
+
+        @pl.when(i == 1)
+        def _():
+            finish(2)
+            leave(0)
+            prepare(1)
+
+        @pl.when(i == 3)
+        def _():
+            leave(1)
+            prepare(2)
+
+        @pl.when(i == 4)
+        def _():
+            open_up(0)
+
+        return 0
+
+    lax.fori_loop(0, 6, body, 0)
+    leave(2)
+    turn_back(0)
+    open_up(1)
+    for rows in blocks:
+        dkeys[rows, :] = (acck[rows, :] * scale).astype(BF)
+        dvalues[rows, :] = accv[rows, :].astype(BF)
+    turn_back(1)
+    close(0)
+    open_up(2)
+    close(1)
+    settle(0)
+    turn_back(2)
+    settle(1)
+    close(2)
+    settle(2)
+    for t in range(3):
+        for cp in core_copies(t) + head_copies(*back0(t)):
+            cp.wait_send()
+        for h in (0, 1):
+            copies = axis_copies(*hop1(t, h)) + axis_copies(*hop2(t, h)) + head_copies(*hop3(t, h))
+            copies += axis_copies(*back1(t, h)) + axis_copies(*back2(t, h)) + [home(t, h)]
+            for cp in copies:
+                cp.wait_send()
+
+
+def mega(info, q, g, k, v, mats, mats_back, keys, values):
+    vm = pl.BlockSpec(memory_space=pltpu.VMEM)
+    sm = pl.BlockSpec(memory_space=pltpu.SMEM)
+    sem = pltpu.SemaphoreType.DMA
+    bf = lambda *shape: pltpu.VMEM(shape, BF)
+    f32 = lambda *shape: pltpu.VMEM(shape, F32)
+    there = [bf(2, 64, 5632), bf(2, 2, 64, 4096)]
+    back = [bf(2, 2, 64, 2048), bf(2, 64, 3584)]
+    home = [bf(2, N_KV, SLOTS, 1024), bf(N_KV, SLOTS, 1792)]
+    hop = [sem((2, 3, 3)), sem((2, 3, 3))]
+    return pl.pallas_call(
+        mega_kernel,
+        out_shape=[
+            jax.ShapeDtypeStruct((3, SLOTS, 8192), BF),
+            jax.ShapeDtypeStruct((3, SLOTS, 1024), BF),
+            jax.ShapeDtypeStruct((3, SLOTS, 1024), BF),
+            jax.ShapeDtypeStruct((PLEN, HD), BF),
+            jax.ShapeDtypeStruct((PLEN, HD), BF),
+        ],
+        in_specs=[sm] + [vm] * 8,
+        out_specs=[vm] * 5,
+        scratch_shapes=[
+            bf(3, SLOTS, 8192), bf(3, SLOTS, 8192), bf(3, SLOTS, 1024), bf(3, SLOTS, 1024),
+            *there, *there, *there, *there,
+            bf(2, N_KV, GROUP, 1408), bf(2, 2, N_KV, GROUP, 1024),
+            bf(2, N_KV, GROUP, 1408), bf(2, 2, N_KV, GROUP, 1024),
+            bf(2, LANES, HD), bf(2, LANES, HD), bf(2, OWN, HD), bf(2, OWN, HD),
+            bf(PLEN // KB, HD, KB),
+            f32(PLEN + OWN, LANES), f32(PLEN + OWN, LANES),
+            f32(PLEN, HD), f32(PLEN, HD), f32(2, OWN, HD), f32(2, OWN, HD),
+            f32(2, LANES, HD),
+            bf(2, N_KV, GROUP, 1024), bf(N_KV, GROUP, 1792),
+            bf(2, N_KV, GROUP, 1024), bf(N_KV, GROUP, 1792),
+            *back, *back, *back, *back, *home, *home,
+            sem((4, 2)), sem((4, 2)), *hop, *hop, sem((2, 3, 7)), sem((2, 3, 7)),
+            sem((3, 7)), sem((3, 7)), *hop, *hop, sem((3, 2)), sem((3, 2)),
+        ],
+        compiler_params=pltpu.CompilerParams(
+            collective_id=0, has_side_effects=True, vmem_limit_bytes=VMEM_BYTES
+        ),
+        name="mega",
+    )(info, q, g, k, v, mats, mats_back, keys, values)
+
+
+def per_device(
+    q_tokens, grad_tokens, roll_keys, roll_values, prompt_keys, prompt_values,
+    slot_prompt, prompt_owner, roll_len, prompt_len,
+):
+    mats, mats_back, info = route_tables(slot_prompt, prompt_owner, roll_len, prompt_len)
+    arrays = (q_tokens, grad_tokens, roll_keys, roll_values)
+
+    def direct():
+        tokens = (jnp.transpose(a, (1, 0, 2)) for a in arrays)
+        gq, gk, gv, dkeys, dvalues = mega(
+            info, *tokens, mats, mats_back, prompt_keys, prompt_values
+        )
+        return (*(jnp.transpose(a, (1, 0, 2)) for a in (gq, gk, gv)), dkeys, dvalues)
+
+    return lax.cond(
+        info[0] > 0,
+        direct,
+        lambda: general(
+            *arrays, prompt_keys, prompt_values, slot_prompt, prompt_owner, roll_len, prompt_len
+        ),
+    )
+
+
 def solution(mesh):
     in_specs = (
         P("roll", "kv", None),

time: 758 us -> 142 us (0.19); the launches traced: 749 us -> 142 us
  local copies, waits for them, and re-layouts: 203 us -> 6.24 us
  waiting for transfers between devices: 178 us -> 0 us
  matrix products: 155 us -> 0 us
  Pallas kernels: 0 us -> 134 us
  other arithmetic: 101 us -> 0.59 us
  starting transfers between devices: 67.3 us -> 0 us
  blocking collectives: 42.8 us -> 0 us
    all_to_all x13 -> x0, waiting for transfers between devices: 178 us -> none  [the longest x1 39.2 us: per_device(): lax.all_to_all(q_back, 'roll', split_axis=0, concat_axis=0, tiled=True)]
    dot_general x80 -> x0, matrix products: 155 us -> none  [the longest x8 33.4 us: step(): jnp.einsum('ntkjd,pkd->ntkjp', grads_b, pvalues, preferred_element_type=f32)]
    pallas_call x0 -> x2, Pallas kernels: none -> 134 us  [the longest x1 131 us: mega(): pl.pallas_call(mega_kernel, out_shape=[jax.ShapeDtypeStruct((3, SLOTS, 81...]
    all_to_all x13 -> x0, starting transfers between devices: 67.3 us -> none  [the longest x1 9.79 us: per_device(): lax.all_to_all(sent_k, 'roll', split_axis=0, concat_axis=0, tiled=True)]
    unnamed x36 -> x7, local copies, waits for them, and re-layouts: 61.5 us -> 6.24 us
    all_to_all x1 -> x0, blocking collectives: 42.8 us -> none  [per_device(): lax.all_to_all(sent_q, 'roll', split_axis=0, concat_axis=0, tiled=True)]
    another operation x21 -> x1, other arithmetic: 37.9 us -> 0.59 us  [route_tables(): jnp.stack([lax.axis_index('roll'), lax.axis_index('kv')]).astype(jnp.int32)]
    all_to_all x11 -> x0, local copies, waits for them, and re-layouts: 34.3 us -> none  [the longest x2 14.1 us: per_device(): lax.all_to_all(q_tokens, 'kv', split_axis=2, concat_axis=1, tiled=True)]
  transfers between devices with their start and end apart: 13 -> 0, of which waited for: 11 -> 0; matrix products, arithmetic and copies ran while one was open for 19% -> 0% of each run, Pallas kernels for 0% -> 0%
where the time goes in v2:
time: 142 us
  Pallas kernels  134 us (94%)
  local copies, waits for them, and re-layouts  6.24 us (4%)
    pallas_call x1, Pallas kernels, mega(): pl.pallas_call(mega_kernel, out_shape=[jax.ShapeDtypeStruct((3, SLOTS, 81...  131 us
    unnamed x7, local copies, waits for them, and re-layouts  6.24 us
    pallas_call x1, Pallas kernels, route_tables(): pl.pallas_call(tables_kernel, out_shape=[jax.ShapeDtypeStruct((2, 5, 64,...  3.41 us

profile of v2, /device:TPU:1, one launch (start us, length us, event | category | flops | bytes accessed | tf_op | source)
XLA Modules:
  0.0 141.7 jit_solution(10051836503784672925)
XLA Ops:
  0.6 0.6 pad_add_fusion.where
  1.2 3.4 %tables.1 = (bf16[2,5,64,64]{3,2,1,0:T(8,128)(2,1)}, bf16[2,4,64,64]{3,2,1,0:T(8,128)(2,1)}, s32[2]{0:T(128)S(1)}) custom-call(s32[2]{0:T(128)} %pad_add_fusion.where, s32[32]{0:T(128)} %owner.1, s32[32]{0:T(128)} %prompt_len.1, s32[1,1024]{1,0:T(1,128)} %bitcast.440, s32[1,1024]{1,0:T(1,128)} %bitcast.441), custom_call_target="tpu_custom_call" | custom-call | tf_op jit(solution)/shard_map/tables/pallas_call | solution.py:358
  4.7 130.8 %conditional.1 = (bf16[32,3,8192]{2,0,1:T(8,128)(2,1)S(1)}, bf16[32,3,1024]{2,0,1:T(8,128)(2,1)S(1)}, bf16[32,3,1024]{2,0,1:T(8,128)(2,1)}, bf16[2048,128]{1,0:T(8,128)(2,1)}, bf16[2048,128]{1,0:T(8,128)(2,1)}) conditional(s32[]{:T(128)} %bitcast.50, (s32[1024]{0:T(1024)}, s32[32]{0:T(128)}, bf16[32,3,8192]{2,0,1:T(8,128)(2,1)}, s32[1024]{0:T(1024)}, ...), branch_computations={%region_0.28_spmd, %region_23.29_spmd} | conditional | flops 1047797248 | bytes 241717472 | solution.py:875
  4.9 130.5 %mega.1 = (bf16[3,32,8192]{2,1,0:T(8,128)(2,1)S(1)}, bf16[3,32,1024]{2,1,0:T(8,128)(2,1)S(1)}, bf16[3,32,1024]{2,1,0:T(8,128)(2,1)}, bf16[2048,128]{1,0:T(8,128)(2,1)}, bf16[2048,128]{1,0:T(8,128)(2,1)}) custom-call(s32[2]{0:T(128)S(1)} %get-tuple-element.132.info, bf16[3,32,8192]{2,1,0:T(8,128)(2,1)} %bitcast.410, bf16[3,32,8192]{2,1,0:T(8,128)(2,1)} %bitcast.411, ...), custom_call_target="tpu_custom_call" | custom-call | tf_op jit(solution)/shard_map/cond/branch_1_fun/mega/pallas_call | solution.py:827
  135.4 0.0 copy-start.18
  135.4 1.1 copy.378
  136.6 0.7 copy.379
  137.3 0.0 copy-done.18
  137.3 0.7 copy.380
  138.0 1.9 %copy.381 = bf16[2048,128]{1,0:T(8,128)(2,1)} copy(bf16[2048,128]{1,0:T(8,128)(2,1)} %get-tuple-element.669) | data formatting | bytes 1048576
  139.8 1.9 %copy.382 = bf16[2048,128]{1,0:T(8,128)(2,1)} copy(bf16[2048,128]{1,0:T(8,128)(2,1)} %get-tuple-element.670) | data formatting | bytes 1048576
Async XLA Ops:
  135.4 1.8 %copy-start.18 = (bf16[32,3,1024]{2,0,1:T(8,128)(2,1)S(1)}, bf16[32,3,1024]{2,0,1:T(8,128)(2,1)}, u32[]{:S(2)}) copy-start(bf16[32,3,1024]{2,0,1:T(8,128)(2,1)} %get-tuple-element.668) | copy-start | bytes 589828

commit v3 on v2

--- a/solution.py
+++ b/solution.py
@@ -249,9 +249,10 @@
 MESH = pl.DeviceIdType.MESH
 BF = jnp.bfloat16
 F32 = jnp.float32
-LANES = 8 * N_KV * HG
+LANES = GROUP * N_KV * HG // 2
 KB = 512
-OWN = 3 * 8 * N_KV
+OWN = RT * GROUP
+OWN_UNIT = 6
 LOG2E = 1.4426950408889634
 VMEM_BYTES = 62 * 1024 * 1024
 
@@ -463,19 +464,26 @@
 
 
 def mega_kernel(
-    info, q, g, k, v, mats, mats_back, keys, values,
+    info, q, g, k, v, mats, mats_back, keys_in, values_in,
     gq, gk, gv, dkeys, dvalues,
-    cq, cg, ck, cv,
-    s1a, s1b, r1a, r1b, s2a, s2b, r2a, r2b, s3a, s3b, za, zb,
-    qs, gs, ko, vo, kt, sc, dp, acck, accv, accok, accov, dqf, da, dl,
-    rza, rzl, b1a, b1l, t1a, t1l, b2a, b2l, t2a, t2l, snda, sndl, rcva, rcvl,
-    core_s, core_r, p1_s, p1_r, p2_s, p2_r, z_s, z_r,
-    y_s, y_r, u1_s, u1_r, u2_s, u2_r, home_s, home_r,
+    oq, og, ok, ov, cq, cg, ck, cv, keys, values,
+    s1a, s1b, r1a, r1b, s2a, s2b, r2a, r2b, s3, s3s, zu, zs,
+    qs, gs, ko, vo, kt, sc, dp, acck, accv, accok, accov, du, dsm, rzu, rzs,
+    b1a, b1l, t1a, t1l, b2a, b2l, t2a, t2l, snda, sndl, rcva, rcvl,
+    own_s, core_s, core_r, p1_s, p1_r, p2_s, p2_r, z_s, z_r, zs_s, zs_r,
+    y_s, y_r, ys_s, ys_r, u1_s, u1_r, u2_s, u2_r, home_s, home_r,
 ):
     place = Place()
-    place.greet()
     scale = HD ** -0.5
     plen = info[1]
+
+    def own_copies(t):
+        names = [(q.at[t], oq.at[t], t, 0), (g.at[t], og.at[t], t, 1)]
+        if t == 0:
+            names += [(k, ok, 3, 0), (v, ov, 3, 1)]
+        if t == 2:
+            names += [(keys_in, keys, 4, 0), (values_in, values, 4, 1)]
+        return [pltpu.make_async_copy(a, b, own_s.at[i, j]) for a, b, i, j in names]
 
     def core_copies(t):
         names = [(q.at[t], cq.at[t], t, 0), (g.at[t], cg.at[t], t, 1)]
@@ -485,26 +493,32 @@
             remote(a, b, core_s.at[i, j], core_r.at[i, j], place.core()) for a, b, i, j in names
         ]
 
-    def part(first, rest, t, h):
-        return first.at[h] if t == 0 else rest.at[h, t - 1]
-
-    def hop1(t, h):
-        return (place, h, part(s1a, s1b, t, h), part(r1a, r1b, t, h), p1_s.at[h, t], p1_r.at[h, t])
-
-    def hop2(t, h):
+    def part(first, rest, u, h):
+        return first.at[h] if u == 1 else rest.at[u - (u > 1), h]
+
+    def hop1(u, h):
+        return (place, h, part(s1a, s1b, u, h), part(r1a, r1b, u, h), p1_s.at[u, h], p1_r.at[u, h])
+
+    def hop2(u, h):
         return (
-            place, 1 - h, part(s2a, s2b, t, h), part(r2a, r2b, t, h), p2_s.at[h, t], p2_r.at[h, t],
-        )
-
-    def hop3(t, h):
-        return (place, part(s3a, s3b, t, h), part(za, zb, t, h), z_s.at[h, t], z_r.at[h, t])
-
-    def pack(t):
-        for cp in core_copies(t):
-            cp.wait_recv()
+            place, 1 - h, part(s2a, s2b, u, h), part(r2a, r2b, u, h), p2_s.at[u, h], p2_r.at[u, h],
+        )
+
+    def hop3(u):
+        return (place, s3.at[u], zu.at[u], z_s.at[u], z_r.at[u])
+
+    small3 = (place, s3s, zs, zs_s, zs_r)
+
+    def pack(u):
+        t, f = u // 2, u % 2
+        if f == 0:
+            for cp in own_copies(t):
+                cp.wait()
+            for cp in core_copies(t):
+                cp.wait_recv()
         for h in (0, 1):
             m = mats[h, 0, :32, :]
-            dst = part(s1a, s1b, t, h)
+            dst = part(s1a, s1b, u, h)
 
             def put(a, b, tt, lo, hi, at):
                 def one(o):
@@ -515,78 +529,61 @@
                 both = jnp.concatenate([one(lo), one(hi)], axis=1).reshape(64, 512)
                 dst[:, pl.ds(at, 512)] = both.astype(BF)
 
-            big, bigo, small, smallo = (q, cq, k, ck) if h == 0 else (g, cg, v, cv)
-
-            def body(i, _):
-                lo = pl.multiple_of(i * 512, 512)
-                put(big, bigo, t, lo, pl.multiple_of(lo + 4096, 512), lo)
-                return 0
-
-            lax.fori_loop(0, 8, body, 0)
-            if t == 0:
+            big, bigo, small, smallo = (oq, cq, ok, ck) if h == 0 else (og, cg, ov, cv)
+            for i in range(4):
+                lo = i * 1024 + f * 512
+                put(big, bigo, t, lo, lo + 4096, i * 512)
+            if u == 1:
                 for tt in range(3):
-                    put(small, smallo, tt, 0, 512, 4096 + tt * 512)
-
-    def send1(t):
+                    put(small, smallo, tt, 0, 512, 2048 + tt * 512)
+
+    def send1(u):
         for h in (0, 1):
-            axis_send(*hop1(t, h))
+            axis_send(*hop1(u, h))
 
     def apply(m, src, dst):
-        def body(i, _):
-            lanes = pl.ds(pl.multiple_of(i * 512, 512), 512)
-            dst[:, lanes] = dot(m, src[:, lanes]).astype(BF)
-            return 0
-
-        lax.fori_loop(0, src.shape[1] // 512, body, 0)
-
-    def turn(t):
+        for o in range(0, src.shape[1], 512):
+            dst[:, o : o + 512] = dot(m, src[:, o : o + 512]).astype(BF)
+
+    def turn(u):
         for h in (0, 1):
-            axis_wait(*hop1(t, h))
-            apply(mats[h, 1], part(r1a, r1b, t, h), part(s2a, s2b, t, h))
-            axis_send(*hop2(t, h))
-
-    def finish(t):
+            axis_wait(*hop1(u, h))
+            apply(mats[h, 1], part(r1a, r1b, u, h), part(s2a, s2b, u, h))
+            axis_send(*hop2(u, h))
+
+    def finish(u):
         for h in (0, 1):
-            axis_wait(*hop2(t, h))
-            m = mats[h, 2 + t, :32, :]
-            src, dst = part(r2a, r2b, t, h), part(s3a, s3b, t, h)
-
-            def body(i, _):
-                o = dot(m, src[:, pl.ds(pl.multiple_of(i * 1024, 1024), 1024)]).astype(BF)
-                dst[i, :, 0:1024] = o[:16]
-                dst[i + 4, :, 0:1024] = o[16:]
-                return 0
-
-            lax.fori_loop(0, 4, body, 0)
-            if t == 0:
+            axis_wait(*hop2(u, h))
+            m = mats[h, 2 + u // 2, :32, :]
+            src = part(r2a, r2b, u, h)
+            for i in range(4):
+                o = dot(m, src[:, i * 512 : (i + 1) * 512]).astype(BF)
+                s3[u, i, h] = o[:16]
+                s3[u, i + 4, h] = o[16:]
+            if u == 1:
                 for tt in range(3):
-                    lo = 4096 + tt * 512
-                    at = 1024 + tt * HD
+                    lo = 2048 + tt * 512
+                    at = slice(tt * HD, (tt + 1) * HD)
                     o = dot(mats[h, 2 + tt, :32, :], src[:, lo : lo + 512]).astype(BF)
                     for i in range(4):
-                        dst[i, :, at : at + HD] = o[:16, i * HD : (i + 1) * HD]
-                        dst[i + 4, :, at : at + HD] = o[16:, i * HD : (i + 1) * HD]
-            head_send(*hop3(t, h))
-
-    def split(block):
-        b = block.astype(F32).reshape(N_KV, 2, 8, HD)
-        return b[:, 0].reshape(64, HD).astype(BF), b[:, 1].reshape(64, HD).astype(BF)
-
-    def prepare(t):
-        for h in (0, 1):
-            head_wait(*hop3(t, h))
-            src, dst = part(za, zb, t, h), (qs, gs)[h]
-            for j in range(HG):
-                a, b = split(src[:, :, j * HD : (j + 1) * HD])
-                dst[0, j * 64 : (j + 1) * 64, :] = a
-                dst[1, j * 64 : (j + 1) * 64, :] = b
-            if t == 0:
-                dst = (ko, vo)[h]
-                for tt in range(3):
-                    at = 1024 + tt * HD
-                    a, b = split(src[:, :, at : at + HD])
-                    dst[0, tt * 64 : (tt + 1) * 64, :] = a
-                    dst[1, tt * 64 : (tt + 1) * 64, :] = b
+                        s3s[i, h, :, at] = o[:16, i * HD : (i + 1) * HD]
+                        s3s[i + 4, h, :, at] = o[16:, i * HD : (i + 1) * HD]
+        head_send(*hop3(u))
+        if u == 1:
+            head_send(*small3)
+
+    def prepare(u):
+        head_wait(*hop3(u))
+        for h, dst in ((0, qs), (1, gs)):
+            for j in range(HG // 2):
+                dst[j * 128 : (j + 1) * 128, :] = zu[u, :, h, :, j * HD : (j + 1) * HD].reshape(128, HD)
+
+    def prepare_own():
+        head_wait(*small3)
+        for h, dst in ((0, ko), (1, vo)):
+            for tt in range(3):
+                at = slice(tt * 128, (tt + 1) * 128)
+                dst[at, :] = zs[:, h, :, at].reshape(128, HD)
 
     def fold_max(s):
         return jnp.max(s.reshape(s.shape[0] // 8, 8, LANES), axis=0)
@@ -597,9 +594,9 @@
     blocks = [slice(b * KB, (b + 1) * KB) for b in range(PLEN // KB)]
     tail = slice(PLEN, PLEN + OWN)
 
-    def chunk(t, e):
-        q_t = jnp.transpose(qs[e].astype(F32)).astype(BF)
-        g_t = jnp.transpose(gs[e].astype(F32)).astype(BF)
+    def chunk(u):
+        q_t = jnp.transpose(qs[...].astype(F32)).astype(BF)
+        g_t = jnp.transpose(gs[...].astype(F32)).astype(BF)
         m8 = jnp.full((8, LANES), -jnp.inf, F32)
         for b, rows in enumerate(blocks):
             s = dot(keys[rows, :], q_t)
@@ -609,10 +606,10 @@
             m8 = jnp.maximum(m8, fold_max(s))
         key = lax.broadcasted_iota(jnp.int32, (OWN, 1), 0)
         lane = lax.broadcasted_iota(jnp.int32, (1, LANES), 1)
-        key_token = 3 * ((key % 64) // 8) + key // 64
-        row_token = 3 * ((lane % 64) // 8) + t
-        same = (key % 8 == lane % 8) & (key_token <= row_token)
-        s = jnp.where(same, dot(ko[e], q_t), -jnp.inf)
+        key_token = 3 * ((key % 128) // GROUP) + key // 128
+        row_token = 3 * ((lane % 128) // GROUP) + u // 2
+        same = (key % GROUP == lane % GROUP) & (key_token <= row_token)
+        s = jnp.where(same, dot(ko[...], q_t), -jnp.inf)
         sc[tail, :] = s
         m8 = jnp.maximum(m8, fold_max(s))
         shift = jnp.max(m8, axis=0, keepdims=True) * (scale * LOG2E)
@@ -621,7 +618,7 @@
         d8 = jnp.zeros((8, LANES), F32)
         for rows in blocks + [tail]:
             w = jnp.exp2(sc[rows, :] * (scale * LOG2E) - shift)
-            d = dot(vo[e] if rows is tail else values[rows, :], g_t)
+            d = dot(vo[...] if rows is tail else values[rows, :], g_t)
             sc[rows, :] = w
             dp[rows, :] = d
             l8 = l8 + fold_sum(w)
@@ -630,200 +627,240 @@
         delta = jnp.sum(d8, axis=0, keepdims=True) * inv
 
         dq = jnp.zeros((HD, LANES), F32)
-        for b, rows in enumerate(blocks + [tail]):
+        for b, rows in enumerate([tail] + blocks):
             p = sc[rows, :] * inv
             ds = (p * (dp[rows, :] - delta)).astype(BF)
             p = p.astype(BF)
             if rows is tail:
-                accov[e] += dot(p, gs[e])
-                accok[e] += dot(ds, qs[e])
-                k_t = jnp.transpose(ko[e].astype(F32)).astype(BF)
+                accov[...] += dot(p, gs[...])
+                accok[...] += dot(ds, qs[...])
+                k_t = jnp.transpose(ko[...].astype(F32)).astype(BF)
             else:
-                accv[rows, :] += dot(p, gs[e])
-                acck[rows, :] += dot(ds, qs[e])
-                k_t = kt[b]
+                accv[rows, :] += dot(p, gs[...])
+                acck[rows, :] += dot(ds, qs[...])
+                k_t = kt[b - 1]
             dq = dq + dot(k_t, ds)
-        dqf[e] = jnp.transpose(dq * scale)
-
-    def joined(pair):
-        a, b = (p.reshape(N_KV, 8, HD) for p in pair)
-        return jnp.concatenate([a, b], axis=1).astype(BF)
-
-    def piece(rest, final, t, *at):
-        return final.at[at] if t == 2 else rest.at[(t, *at)]
-
-    def back0(t):
+            if rows is tail:
+                pl.when(u == 5)(leave_own)
+        dq = jnp.transpose(dq * scale).astype(BF)
+        for j in range(HG // 2):
+            du[u, :, :, j * HD : (j + 1) * HD] = dq[j * 128 : (j + 1) * 128, :].reshape(N_KV, GROUP, HD)
+
+    def piece(rest, final, u, *at):
+        return final.at[at] if u == OWN_UNIT else rest.at[(u, *at)]
+
+    def back0(u):
+        return (place, du.at[u], rzu.at[u], y_s.at[u], y_r.at[u])
+
+    small0 = (place, dsm, rzs, ys_s, ys_r)
+
+    def back1(u, h):
         return (
-            place, dl if t == 2 else da.at[t], rzl if t == 2 else rza.at[t], y_s.at[t], y_r.at[t],
-        )
-
-    def back1(t, h):
+            place, 1 - h, piece(b1a, b1l, u, h), piece(t1a, t1l, u, h), u1_s.at[u, h], u1_r.at[u, h],
+        )
+
+    def back2(u, h):
         return (
-            place, 1 - h, piece(b1a, b1l, t, h), piece(t1a, t1l, t, h), u1_s.at[h, t], u1_r.at[h, t],
-        )
-
-    def back2(t, h):
-        return (
-            place, h, piece(b2a, b2l, t, h), piece(t2a, t2l, t, h), u2_s.at[h, t], u2_r.at[h, t],
-        )
-
-    def home(t, h):
+            place, h, piece(b2a, b2l, u, h), piece(t2a, t2l, u, h), u2_s.at[u, h], u2_r.at[u, h],
+        )
+
+    def home(u, h):
         heads = pl.ds(4 * h, 4)
         return remote(
-            piece(snda, sndl, t, heads), piece(rcva, rcvl, t, heads),
-            home_s.at[t, h], home_r.at[t, h], place.core(),
-        )
-
-    def leave(t):
-        dst = dl if t == 2 else da.at[t]
-        for j in range(HG):
-            rows = slice(j * 64, (j + 1) * 64)
-            dst[:, :, j * HD : (j + 1) * HD] = joined((dqf[0, rows, :], dqf[1, rows, :]))
-        if t == 2:
-            for tt in range(3):
-                rows = slice(tt * 64, (tt + 1) * 64)
-                at = 1024 + tt * HD
-                dst[:, :, at : at + HD] = joined((accok[0, rows, :] * scale, accok[1, rows, :] * scale))
-                dst[:, :, at + 384 : at + 384 + HD] = joined((accov[0, rows, :], accov[1, rows, :]))
-        head_send(*back0(t))
-
-    def open_up(t):
-        head_wait(*back0(t))
-        src = rzl if t == 2 else rza.at[t]
-        wide, step = (1792, 896) if t == 2 else (1024, 512)
+            piece(snda, sndl, u, heads), piece(rcva, rcvl, u, heads),
+            home_s.at[u, h], home_r.at[u, h], place.core(),
+        )
+
+    def leave_own():
+        for tt in range(3):
+            at = slice(tt * 128, (tt + 1) * 128)
+            dsm[:, :, at] = (accok[at, :] * scale).astype(BF).reshape(N_KV, GROUP, HD)
+            dsm[:, :, 384 + tt * 128 : 512 + tt * 128] = accov[at, :].astype(BF).reshape(N_KV, GROUP, HD)
+        head_send(*small0)
+
+    def open_up(u):
+        head_wait(*(small0 if u == OWN_UNIT else back0(u)))
+        src = rzs if u == OWN_UNIT else rzu.at[u]
+        wide = src.shape[-1]
         for h in (0, 1):
             m = mats_back[h, 3, :, :32]
-            dst = piece(b1a, b1l, t, h)
+            dst = piece(b1a, b1l, u, h)
             for lo in (0, 1):
-                for o in range(0, wide, step):
-                    rows = jnp.concatenate(
-                        [src[h * 4 + lo, :, o : o + step], src[h * 4 + 2 + lo, :, o : o + step]], axis=0
-                    )
-                    dst[:, lo * wide + o : lo * wide + o + step] = dot(m, rows).astype(BF)
-            axis_send(*back1(t, h))
-
-    def turn_back(t):
+                rows = jnp.concatenate([src[h * 4 + lo], src[h * 4 + 2 + lo]], axis=0)
+                dst[:, lo * wide : (lo + 1) * wide] = dot(m, rows).astype(BF)
+            axis_send(*back1(u, h))
+
+    def turn_back(u):
         for h in (0, 1):
-            axis_wait(*back1(t, h))
-            apply(mats_back[h, 2], piece(t1a, t1l, t, h), piece(b2a, b2l, t, h))
-            axis_send(*back2(t, h))
-
-    def close(t):
-        wide = 1792 if t == 2 else 1024
+            axis_wait(*back1(u, h))
+            apply(mats_back[h, 2], piece(t1a, t1l, u, h), piece(b2a, b2l, u, h))
+            axis_send(*back2(u, h))
+
+    def close(u):
+        t, f = u // 2, u % 2
         for h in (0, 1):
-            axis_wait(*back2(t, h))
-            src = piece(t2a, t2l, t, h)
+            axis_wait(*back2(u, h))
+            src = piece(t2a, t2l, u, h)
+            wide = src.shape[-1] // 2
             for hh in (0, 1):
                 m = mats_back[h, hh]
                 for lo in (0, 1):
                     c = h * 4 + hh * 2 + lo
-                    snd = piece(snda, sndl, t, c)
-                    for o in (0, 512):
-                        r = dot(m, src[:, lo * wide + o : lo * wide + o + 512]).astype(BF)
-                        gq[t, :, c * 1024 + o : c * 1024 + o + 512] = r[:32]
-                        snd[:, o : o + 512] = r[32:]
-                    if t == 2:
-                        r = dot(m, src[:, lo * wide + 1024 : (lo + 1) * wide]).astype(BF)
-                        snd[:, 1024:1792] = r[32:]
+                    r = dot(m, src[:, lo * wide : (lo + 1) * wide]).astype(BF)
+                    piece(snda, sndl, u, c)[...] = r[32:]
+                    if u == OWN_UNIT:
+                        lanes = slice(c * HD, (c + 1) * HD)
                         for tt in range(3):
-                            lanes = slice(c * HD, (c + 1) * HD)
                             gk[tt, :, lanes] = r[:32, tt * HD : (tt + 1) * HD]
                             gv[tt, :, lanes] = r[:32, 384 + tt * HD : 384 + (tt + 1) * HD]
-            home(t, h).start()
-
-    def settle(t):
+                    else:
+                        at = c * 1024 + f * 512
+                        gq[t, :, at : at + 512] = r[:32]
+            home(u, h).start()
+
+    def settle(u):
+        t, f = u // 2, u % 2
         for h in (0, 1):
-            home(t, h).wait_recv()
-        src = rcvl if t == 2 else rcva.at[t]
+            home(u, h).wait_recv()
+        src = rcvl if u == OWN_UNIT else rcva.at[u]
         for c in range(N_KV):
-            lanes = slice(c * 1024, (c + 1) * 1024)
-            gq[t, :, lanes] = gq[t, :, lanes] + src[c, :, 0:1024]
-            if t == 2:
+            if u == OWN_UNIT:
                 lanes = slice(c * HD, (c + 1) * HD)
                 for tt in range(3):
-                    at = 1024 + tt * HD
+                    at = tt * HD
                     gk[tt, :, lanes] = gk[tt, :, lanes] + src[c, :, at : at + HD]
                     gv[tt, :, lanes] = gv[tt, :, lanes] + src[c, :, at + 384 : at + 384 + HD]
+            else:
+                lanes = slice(c * 1024 + f * 512, c * 1024 + f * 512 + 512)
+                gq[t, :, lanes] = gq[t, :, lanes] + src[c]
+
+    def start(copies):
+        for cp in copies:
+            cp.start()
 
     for t in range(3):
-        for cp in core_copies(t):
-            cp.start()
+        start(own_copies(t))
+    place.greet()
+    start(core_copies(0))
     pack(0)
     send1(0)
+    start(core_copies(1))
     pack(1)
     turn(0)
     send1(1)
     pack(2)
+    send1(2)
+    start(core_copies(2))
     finish(0)
     turn(1)
-    send1(2)
+    pack(3)
+    send1(3)
+    finish(1)
+    turn(2)
+    pack(4)
+    send1(4)
     for b, rows in enumerate(blocks):
         kt[b] = jnp.transpose(keys[rows, :].astype(F32)).astype(BF)
     for ref in (acck, accv, accok, accov):
         ref[...] = jnp.zeros_like(ref)
-    finish(1)
-    prepare(0)
+    finish(2)
+    turn(3)
+    pack(5)
+    send1(5)
+    prepare_own()
 
     def body(i, _):
-        chunk(i // 2, i % 2)
+        prepare(i)
+        chunk(i)
+        head_send(*back0(i))
 
         @pl.when(i == 0)
         def _():
-            turn(2)
+            finish(3)
+            turn(4)
 
         @pl.when(i == 1)
         def _():
-            finish(2)
-            leave(0)
-            prepare(1)
+            finish(4)
+            turn(5)
+
+        @pl.when(i == 2)
+        def _():
+            finish(5)
+            open_up(0)
 
         @pl.when(i == 3)
         def _():
-            leave(1)
-            prepare(2)
+            open_up(1)
+            turn_back(0)
 
         @pl.when(i == 4)
         def _():
-            open_up(0)
+            open_up(2)
+            turn_back(1)
+            close(0)
 
         return 0
 
     lax.fori_loop(0, 6, body, 0)
-    leave(2)
-    turn_back(0)
-    open_up(1)
+    open_up(3)
+    turn_back(2)
+    close(1)
+    open_up(4)
+    settle(0)
+    turn_back(3)
+    close(2)
+    settle(1)
     for rows in blocks:
         dkeys[rows, :] = (acck[rows, :] * scale).astype(BF)
         dvalues[rows, :] = accv[rows, :].astype(BF)
-    turn_back(1)
-    close(0)
-    open_up(2)
-    close(1)
-    settle(0)
-    turn_back(2)
-    settle(1)
-    close(2)
+    open_up(OWN_UNIT)
+    turn_back(4)
+    open_up(5)
+    turn_back(OWN_UNIT)
+    close(3)
     settle(2)
+    turn_back(5)
+    close(4)
+    settle(3)
+    close(OWN_UNIT)
+    settle(4)
+    close(5)
+    settle(OWN_UNIT)
+    settle(5)
     for t in range(3):
-        for cp in core_copies(t) + head_copies(*back0(t)):
+        for cp in core_copies(t):
             cp.wait_send()
+    for cp in head_copies(*small3) + head_copies(*small0):
+        cp.wait_send()
+    for u in range(7):
+        copies = []
+        if u < 6:
+            copies += head_copies(*hop3(u)) + head_copies(*back0(u))
         for h in (0, 1):
-            copies = axis_copies(*hop1(t, h)) + axis_copies(*hop2(t, h)) + head_copies(*hop3(t, h))
-            copies += axis_copies(*back1(t, h)) + axis_copies(*back2(t, h)) + [home(t, h)]
-            for cp in copies:
-                cp.wait_send()
+            if u < 6:
+                copies += axis_copies(*hop1(u, h)) + axis_copies(*hop2(u, h))
+            copies += axis_copies(*back1(u, h)) + axis_copies(*back2(u, h)) + [home(u, h)]
+        for cp in copies:
+            cp.wait_send()
 
 
 def mega(info, q, g, k, v, mats, mats_back, keys, values):
     vm = pl.BlockSpec(memory_space=pltpu.VMEM)
     sm = pl.BlockSpec(memory_space=pltpu.SMEM)
+    hbm = pl.BlockSpec(memory_space=pl.ANY)
     sem = pltpu.SemaphoreType.DMA
     bf = lambda *shape: pltpu.VMEM(shape, BF)
     f32 = lambda *shape: pltpu.VMEM(shape, F32)
-    there = [bf(2, 64, 5632), bf(2, 2, 64, 4096)]
-    back = [bf(2, 2, 64, 2048), bf(2, 64, 3584)]
-    home = [bf(2, N_KV, SLOTS, 1024), bf(N_KV, SLOTS, 1792)]
-    hop = [sem((2, 3, 3)), sem((2, 3, 3))]
+    rows = [
+        bf(3, SLOTS, 8192), bf(3, SLOTS, 8192), bf(3, SLOTS, 1024), bf(3, SLOTS, 1024),
+    ]
+    there = [bf(2, 64, 3584), bf(5, 2, 64, 2048)]
+    back = [bf(6, 2, 64, 1024), bf(2, 64, 1536)]
+    home = [bf(6, N_KV, SLOTS, 512), bf(N_KV, SLOTS, 768)]
+    hop_back = [sem((7, 2, 3)), sem((7, 2, 3))]
+    hop = [sem((6, 2, 3)), sem((6, 2, 3))]
+    head = [sem((6, 7)), sem((6, 7)), sem((7,)), sem((7,))]
     return pl.pallas_call(
         mega_kernel,
         out_shape=[
@@ -833,23 +870,22 @@
             jax.ShapeDtypeStruct((PLEN, HD), BF),
             jax.ShapeDtypeStruct((PLEN, HD), BF),
         ],
-        in_specs=[sm] + [vm] * 8,
+        in_specs=[sm] + [hbm] * 4 + [vm] * 2 + [hbm] * 2,
         out_specs=[vm] * 5,
         scratch_shapes=[
-            bf(3, SLOTS, 8192), bf(3, SLOTS, 8192), bf(3, SLOTS, 1024), bf(3, SLOTS, 1024),
+            *rows, *rows, bf(PLEN, HD), bf(PLEN, HD),
             *there, *there, *there, *there,
-            bf(2, N_KV, GROUP, 1408), bf(2, 2, N_KV, GROUP, 1024),
-            bf(2, N_KV, GROUP, 1408), bf(2, 2, N_KV, GROUP, 1024),
-            bf(2, LANES, HD), bf(2, LANES, HD), bf(2, OWN, HD), bf(2, OWN, HD),
+            bf(6, N_KV, 2, GROUP, 512), bf(N_KV, 2, GROUP, 384),
+            bf(6, N_KV, 2, GROUP, 512), bf(N_KV, 2, GROUP, 384),
+            bf(LANES, HD), bf(LANES, HD), bf(OWN, HD), bf(OWN, HD),
             bf(PLEN // KB, HD, KB),
             f32(PLEN + OWN, LANES), f32(PLEN + OWN, LANES),
-            f32(PLEN, HD), f32(PLEN, HD), f32(2, OWN, HD), f32(2, OWN, HD),
-            f32(2, LANES, HD),
-            bf(2, N_KV, GROUP, 1024), bf(N_KV, GROUP, 1792),
-            bf(2, N_KV, GROUP, 1024), bf(N_KV, GROUP, 1792),
+            f32(PLEN, HD), f32(PLEN, HD), f32(OWN, HD), f32(OWN, HD),
+            bf(6, N_KV, GROUP, 512), bf(N_KV, GROUP, 768),
+            bf(6, N_KV, GROUP, 512), bf(N_KV, GROUP, 768),
             *back, *back, *back, *back, *home, *home,
-            sem((4, 2)), sem((4, 2)), *hop, *hop, sem((2, 3, 7)), sem((2, 3, 7)),
-            sem((3, 7)), sem((3, 7)), *hop, *hop, sem((3, 2)), sem((3, 2)),
+            sem((5, 2)), sem((4, 2)), sem((4, 2)), *hop, *hop, *head,
+            *head, *hop_back, *hop_back, sem((7, 2)), sem((7, 2)),
         ],
         compiler_params=pltpu.CompilerParams(
             collective_id=0, has_side_effects=True, vmem_limit_bytes=VMEM_BYTES

time: 142 us -> 130 us (0.915)
  Pallas kernels: 134 us -> 122 us
    pallas_call x1, Pallas kernels: 131 us -> 119 us  [mega(): pl.pallas_call(mega_kernel, out_shape=[jax.ShapeDtypeStruct((3, SLOTS, 81...]
where the time goes in v3:
time: 130 us
  Pallas kernels  122 us (94%)
  local copies, waits for them, and re-layouts  6.24 us (5%)
    pallas_call x1, Pallas kernels, mega(): pl.pallas_call(mega_kernel, out_shape=[jax.ShapeDtypeStruct((3, SLOTS, 81...  119 us
    unnamed x7, local copies, waits for them, and re-layouts  6.24 us
    pallas_call x1, Pallas kernels, route_tables(): pl.pallas_call(tables_kernel, out_shape=[jax.ShapeDtypeStruct((2, 5, 64,...  3.41 us

profile of v3, /device:TPU:1, one launch (start us, length us, event | category | flops | bytes accessed | tf_op | source)
XLA Modules:
  0.0 130.1 jit_solution(17022384388707804626)
XLA Ops:
  0.6 0.6 pad_add_fusion.where
  1.2 3.4 %tables.1 = (bf16[2,5,64,64]{3,2,1,0:T(8,128)(2,1)}, bf16[2,4,64,64]{3,2,1,0:T(8,128)(2,1)}, s32[2]{0:T(128)S(1)}) custom-call(s32[2]{0:T(128)} %pad_add_fusion.where, s32[32]{0:T(128)} %owner.1, s32[32]{0:T(128)} %prompt_len.1, s32[1,1024]{1,0:T(1,128)} %bitcast.440, s32[1,1024]{1,0:T(1,128)} %bitcast.441), custom_call_target="tpu_custom_call" | custom-call | tf_op jit(solution)/shard_map/tables/pallas_call | solution.py:359
  4.7 119.2 %conditional.1 = (bf16[32,3,8192]{2,0,1:T(8,128)(2,1)S(1)}, bf16[32,3,1024]{2,0,1:T(8,128)(2,1)S(1)}, bf16[32,3,1024]{2,0,1:T(8,128)(2,1)}, bf16[2048,128]{1,0:T(8,128)(2,1)}, bf16[2048,128]{1,0:T(8,128)(2,1)}) conditional(s32[]{:T(128)} %bitcast.50, (s32[1024]{0:T(1024)}, s32[32]{0:T(128)}, bf16[32,3,8192]{2,0,1:T(8,128)(2,1)}, s32[1024]{0:T(1024)}, ...), branch_computations={%region_0.28_spmd, %region_23.29_spmd} | conditional | flops 1047797248 | bytes 241717472 | solution.py:911
  4.9 118.7 %mega.1 = (bf16[3,32,8192]{2,1,0:T(8,128)(2,1)S(1)}, bf16[3,32,1024]{2,1,0:T(8,128)(2,1)S(1)}, bf16[3,32,1024]{2,1,0:T(8,128)(2,1)}, bf16[2048,128]{1,0:T(8,128)(2,1)}, bf16[2048,128]{1,0:T(8,128)(2,1)}) custom-call(s32[2]{0:T(128)S(1)} %get-tuple-element.132.info, bf16[3,32,8192]{2,1,0:T(8,128)(2,1)} %bitcast.410, bf16[3,32,8192]{2,1,0:T(8,128)(2,1)} %bitcast.411, ...), custom_call_target="tpu_custom_call" | custom-call | tf_op jit(solution)/shard_map/cond/branch_1_fun/mega/pallas_call | solution.py:864
  123.9 0.0 copy-start.18
  123.9 1.1 copy.378
  125.0 0.7 copy.379
  125.7 0.0 copy-done.18
  125.7 0.7 copy.380
  126.4 1.9 %copy.381 = bf16[2048,128]{1,0:T(8,128)(2,1)} copy(bf16[2048,128]{1,0:T(8,128)(2,1)} %get-tuple-element.669) | data formatting | bytes 1048576
  128.3 1.9 %copy.382 = bf16[2048,128]{1,0:T(8,128)(2,1)} copy(bf16[2048,128]{1,0:T(8,128)(2,1)} %get-tuple-element.670) | data formatting | bytes 1048576
Async XLA Ops:
  123.9 1.8 %copy-start.18 = (bf16[32,3,1024]{2,0,1:T(8,128)(2,1)S(1)}, bf16[32,3,1024]{2,0,1:T(8,128)(2,1)}, u32[]{:S(2)}) copy-start(bf16[32,3,1024]{2,0,1:T(8,128)(2,1)} %get-tuple-element.668) | copy-start | bytes 589828

commit v4 on v3

--- a/solution.py
+++ b/solution.py
@@ -328,7 +328,7 @@
         mats[h, 0] = dot_t(marks(jnp.where(near, d1 * CAP + first[h], -1), 64).astype(BF), seat).astype(BF)
         turn = jnp.zeros((64, 64), F32)
         turn_back = jnp.zeros((64, 64), F32)
-        ends = [jnp.zeros((64, 64), F32)] * 3
+        ends = [jnp.zeros((64, 64), F32)] * 8
         end_back = jnp.zeros((64, 64), F32)
         for part in (0, 1):
             mats_back[h, part] = dot_t(seat, wide(d1, first[h], near, part)).astype(BF)
@@ -338,15 +338,17 @@
             a = wide(s2, second[h], mine, part)
             b = marks(jnp.where(mine, part * GROUP + last, -1), 64).astype(BF)
             end_back = end_back + dot_t(a, b)
-            for t in range(3):
-                if h == 0:
-                    ends[t] = ends[t] + dot_t(b, a)
-                else:
-                    valid = mine & (3 * kv + t < lens[...])
+            ends[3] = ends[3] + dot_t(b, a)
+            if h == 0:
+                continue
+            tokens = [3 * kv, 3 * kv + 1, 3 * kv + 2, None] + [12 * part + 3 * i + 2 for i in range(4)]
+            for t, token in enumerate(tokens):
+                if token is not None:
+                    valid = mine & (token < lens[...])
                     b = marks(jnp.where(valid, part * GROUP + last, -1), 64).astype(BF)
                     ends[t] = ends[t] + dot_t(b, a)
         mats[h, 1] = turn.astype(BF)
-        for t in range(3):
+        for t in range(8):
             mats[h, 2 + t] = ends[t].astype(BF)
         mats_back[h, 2] = turn_back.astype(BF)
         mats_back[h, 3] = end_back.astype(BF)
@@ -359,7 +361,7 @@
     return pl.pallas_call(
         tables_kernel,
         out_shape=[
-            jax.ShapeDtypeStruct((2, 5, 64, 64), BF),
+            jax.ShapeDtypeStruct((2, 10, 64, 64), BF),
             jax.ShapeDtypeStruct((2, 4, 64, 64), BF),
             jax.ShapeDtypeStruct((2,), jnp.int32),
         ],
@@ -466,11 +468,11 @@
 def mega_kernel(
     info, q, g, k, v, mats, mats_back, keys_in, values_in,
     gq, gk, gv, dkeys, dvalues,
-    oq, og, ok, ov, cq, cg, ck, cv, keys, values,
-    s1a, s1b, r1a, r1b, s2a, s2b, r2a, r2b, s3, s3s, zu, zs,
+    oq, og, zk, zv, zq5, zg5, cq, cg, ck, cv, cq5, cg5, keys, values,
+    s1a, s1b, r1a, r1b, s2a, s2b, r2a, r2b, s3, zu,
     qs, gs, ko, vo, kt, sc, dp, acck, accv, accok, accov, du, dsm, rzu, rzs,
     b1a, b1l, t1a, t1l, b2a, b2l, t2a, t2l, snda, sndl, rcva, rcvl,
-    own_s, core_s, core_r, p1_s, p1_r, p2_s, p2_r, z_s, z_r, zs_s, zs_r,
+    own_s, early_o, early_s, early_r, core_s, core_r, p1_s, p1_r, p2_s, p2_r, z_s, z_r,
     y_s, y_r, ys_s, ys_r, u1_s, u1_r, u2_s, u2_r, home_s, home_r,
 ):
     place = Place()
@@ -479,22 +481,50 @@
 
     def own_copies(t):
         names = [(q.at[t], oq.at[t], t, 0), (g.at[t], og.at[t], t, 1)]
-        if t == 0:
-            names += [(k, ok, 3, 0), (v, ov, 3, 1)]
         if t == 2:
-            names += [(keys_in, keys, 4, 0), (values_in, values, 4, 1)]
+            names += [(keys_in, keys, 3, 0), (values_in, values, 3, 1)]
         return [pltpu.make_async_copy(a, b, own_s.at[i, j]) for a, b, i, j in names]
 
     def core_copies(t):
-        names = [(q.at[t], cq.at[t], t, 0), (g.at[t], cg.at[t], t, 1)]
-        if t == 0:
-            names += [(k, ck, 3, 0), (v, cv, 3, 1)]
+        a, b, c, d = ((zk, ck, zv, cv), (zq5, cq5, zg5, cg5))[t - 3] if t > 2 else (
+            q.at[t], cq.at[t], g.at[t], cg.at[t]
+        )
         return [
-            remote(a, b, core_s.at[i, j], core_r.at[i, j], place.core()) for a, b, i, j in names
+            remote(a, b, core_s.at[t, 0], core_r.at[t, 0], place.core()),
+            remote(c, d, core_s.at[t, 1], core_r.at[t, 1], place.core()),
         ]
 
+    def lanes(at, size):
+        return pl.ds(pl.multiple_of(at, size), size)
+
+    def early(j, c, p):
+        if j < 2:
+            return (k, v)[j].at[:, :, lanes(c * HD, HD)], (zk, zv)[j].at[:, :, lanes(p * HD, HD)]
+        src, dst = ((q, zq5), (g, zg5))[j - 2]
+        return (
+            src.at[2, :, lanes(c * 1024 + 512, 512)], dst.at[0, :, lanes(p * 512, 512)],
+        )
+
+    def early_copies(j):
+        copies = []
+        for i in (4, 3, 5, 2, 6, 1, 7):
+            a, b = early(j, (place.kv + i) % N_KV, place.kv)
+            copies.append(remote(a, b, early_s.at[j, i - 1], early_r.at[j, i - 1], place.head(i)))
+        return copies
+
+    def early_own(j):
+        a, b = early(j, place.kv, place.kv)
+        return pltpu.make_async_copy(a, b, early_o.at[j])
+
+    def early_wait(j):
+        for i in range(1, N_KV):
+            c = (place.kv - i + N_KV) % N_KV
+            a, b = early(j, c, c)
+            remote(a, b, early_s.at[j, i - 1], early_r.at[j, i - 1], place.head(i)).wait_recv()
+        early_own(j).wait()
+
     def part(first, rest, u, h):
-        return first.at[h] if u == 1 else rest.at[u - (u > 1), h]
+        return first.at[h] if u == 2 else rest.at[u - (u > 2), h]
 
     def hop1(u, h):
         return (place, h, part(s1a, s1b, u, h), part(r1a, r1b, u, h), p1_s.at[u, h], p1_r.at[u, h])
@@ -506,16 +536,19 @@
 
     def hop3(u):
         return (place, s3.at[u], zu.at[u], z_s.at[u], z_r.at[u])
-
-    small3 = (place, s3s, zs, zs_s, zs_r)
 
     def pack(u):
         t, f = u // 2, u % 2
         if f == 0:
             for cp in own_copies(t):
                 cp.wait()
-            for cp in core_copies(t):
-                cp.wait_recv()
+        arrived = core_copies(t) if f == 0 else []
+        if u == 2:
+            arrived += core_copies(3)
+        if u == 5:
+            arrived += core_copies(4)
+        for cp in arrived:
+            cp.wait_recv()
         for h in (0, 1):
             m = mats[h, 0, :32, :]
             dst = part(s1a, s1b, u, h)
@@ -529,11 +562,14 @@
                 both = jnp.concatenate([one(lo), one(hi)], axis=1).reshape(64, 512)
                 dst[:, pl.ds(at, 512)] = both.astype(BF)
 
-            big, bigo, small, smallo = (oq, cq, ok, ck) if h == 0 else (og, cg, ov, cv)
+            big, bigo, small, smallo = (oq, cq, zk, ck) if h == 0 else (og, cg, zv, cv)
             for i in range(4):
                 lo = i * 1024 + f * 512
-                put(big, bigo, t, lo, lo + 4096, i * 512)
-            if u == 1:
+                if u == 5:
+                    put((zq5, zg5)[h], (cq5, cg5)[h], 0, i * 512, 2048 + i * 512, i * 512)
+                else:
+                    put(big, bigo, t, lo, lo + 4096, i * 512)
+            if u == 2:
                 for tt in range(3):
                     put(small, smallo, tt, 0, 512, 2048 + tt * 512)
 
@@ -554,36 +590,30 @@
     def finish(u):
         for h in (0, 1):
             axis_wait(*hop2(u, h))
-            m = mats[h, 2 + u // 2, :32, :]
             src = part(r2a, r2b, u, h)
             for i in range(4):
-                o = dot(m, src[:, i * 512 : (i + 1) * 512]).astype(BF)
-                s3[u, i, h] = o[:16]
-                s3[u, i + 4, h] = o[16:]
-            if u == 1:
+                m = 5 if h == 0 else 6 + i if u == 5 else 2 + u // 2
+                o = dot(mats[h, m, :32, :], src[:, i * 512 : (i + 1) * 512]).astype(BF)
+                dst = zu if u == 5 else s3
+                dst[u, i, h] = o[:16]
+                dst[u, i + 4, h] = o[16:]
+            if u == 2:
+                dst = (ko, vo)[h]
                 for tt in range(3):
                     lo = 2048 + tt * 512
-                    at = slice(tt * HD, (tt + 1) * HD)
-                    o = dot(mats[h, 2 + tt, :32, :], src[:, lo : lo + 512]).astype(BF)
+                    o = dot(mats[h, 5, :32, :], src[:, lo : lo + 512]).astype(BF)
                     for i in range(4):
-                        s3s[i, h, :, at] = o[:16, i * HD : (i + 1) * HD]
-                        s3s[i + 4, h, :, at] = o[16:, i * HD : (i + 1) * HD]
-        head_send(*hop3(u))
-        if u == 1:
-            head_send(*small3)
+                        at = tt * 128 + i * GROUP
+                        dst[at : at + GROUP, :] = o[:16, i * HD : (i + 1) * HD]
+                        dst[at + 64 : at + 64 + GROUP, :] = o[16:, i * HD : (i + 1) * HD]
+        if u < 5:
+            head_send(*hop3(u))
 
     def prepare(u):
-        head_wait(*hop3(u))
+        pl.when(u < 5)(lambda: head_wait(*hop3(u)))
         for h, dst in ((0, qs), (1, gs)):
             for j in range(HG // 2):
                 dst[j * 128 : (j + 1) * 128, :] = zu[u, :, h, :, j * HD : (j + 1) * HD].reshape(128, HD)
-
-    def prepare_own():
-        head_wait(*small3)
-        for h, dst in ((0, ko), (1, vo)):
-            for tt in range(3):
-                at = slice(tt * 128, (tt + 1) * 128)
-                dst[at, :] = zs[:, h, :, at].reshape(128, HD)
 
     def fold_max(s):
         return jnp.max(s.reshape(s.shape[0] // 8, 8, LANES), axis=0)
@@ -600,8 +630,9 @@
         m8 = jnp.full((8, LANES), -jnp.inf, F32)
         for b, rows in enumerate(blocks):
             s = dot(keys[rows, :], q_t)
-            seen = lax.broadcasted_iota(jnp.int32, (KB, 1), 0) + b * KB < plen
-            s = jnp.where(seen, s, -jnp.inf)
+            if b > 0:
+                seen = lax.broadcasted_iota(jnp.int32, (KB, 1), 0) + b * KB < plen
+                s = jnp.where(seen, s, -jnp.inf)
             sc[rows, :] = s
             m8 = jnp.maximum(m8, fold_max(s))
         key = lax.broadcasted_iota(jnp.int32, (OWN, 1), 0)
@@ -641,7 +672,7 @@
                 k_t = kt[b - 1]
             dq = dq + dot(k_t, ds)
             if rows is tail:
-                pl.when(u == 5)(leave_own)
+                pl.when(u == 4)(leave_own)
         dq = jnp.transpose(dq * scale).astype(BF)
         for j in range(HG // 2):
             du[u, :, :, j * HD : (j + 1) * HD] = dq[j * 128 : (j + 1) * 128, :].reshape(N_KV, GROUP, HD)
@@ -742,19 +773,28 @@
         start(own_copies(t))
     place.greet()
     start(core_copies(0))
+    for j in range(4):
+        early_own(j).start()
+        start(early_copies(j))
     pack(0)
     send1(0)
     start(core_copies(1))
     pack(1)
     turn(0)
     send1(1)
+    early_wait(0)
+    early_wait(1)
+    start(core_copies(3))
+    start(core_copies(2))
+    finish(0)
     pack(2)
     send1(2)
-    start(core_copies(2))
-    finish(0)
     turn(1)
     pack(3)
     send1(3)
+    early_wait(2)
+    early_wait(3)
+    start(core_copies(4))
     finish(1)
     turn(2)
     pack(4)
@@ -767,12 +807,13 @@
     turn(3)
     pack(5)
     send1(5)
-    prepare_own()
 
     def body(i, _):
-        prepare(i)
-        chunk(i)
-        head_send(*back0(i))
+        late = i // 3
+        u = (1 - late) * i + late * (3 + (i + 2) % 3)
+        prepare(u)
+        chunk(u)
+        head_send(*back0(u))
 
         @pl.when(i == 0)
         def _():
@@ -799,44 +840,49 @@
             open_up(2)
             turn_back(1)
             close(0)
+            open_up(5)
 
         return 0
 
     lax.fori_loop(0, 6, body, 0)
+    turn_back(2)
     open_up(3)
-    turn_back(2)
     close(1)
-    open_up(4)
     settle(0)
-    turn_back(3)
+    turn_back(5)
     close(2)
     settle(1)
     for rows in blocks:
         dkeys[rows, :] = (acck[rows, :] * scale).astype(BF)
         dvalues[rows, :] = accv[rows, :].astype(BF)
+    turn_back(3)
     open_up(OWN_UNIT)
-    turn_back(4)
-    open_up(5)
+    close(5)
+    settle(2)
+    open_up(4)
     turn_back(OWN_UNIT)
     close(3)
-    settle(2)
-    turn_back(5)
+    settle(5)
+    turn_back(4)
+    close(OWN_UNIT)
+    settle(3)
     close(4)
-    settle(3)
-    close(OWN_UNIT)
+    settle(OWN_UNIT)
     settle(4)
-    close(5)
-    settle(OWN_UNIT)
-    settle(5)
-    for t in range(3):
+    for t in range(5):
         for cp in core_copies(t):
             cp.wait_send()
-    for cp in head_copies(*small3) + head_copies(*small0):
+    for j in range(4):
+        for cp in early_copies(j):
+            cp.wait_send()
+    for cp in head_copies(*small0):
         cp.wait_send()
     for u in range(7):
         copies = []
         if u < 6:
-            copies += head_copies(*hop3(u)) + head_copies(*back0(u))
+            copies += head_copies(*back0(u))
+        if u < 5:
+            copies += head_copies(*hop3(u))
         for h in (0, 1):
             if u < 6:
                 copies += axis_copies(*hop1(u, h)) + axis_copies(*hop2(u, h))
@@ -854,6 +900,7 @@
     f32 = lambda *shape: pltpu.VMEM(shape, F32)
     rows = [
         bf(3, SLOTS, 8192), bf(3, SLOTS, 8192), bf(3, SLOTS, 1024), bf(3, SLOTS, 1024),
+        bf(1, SLOTS, 4096), bf(1, SLOTS, 4096),
     ]
     there = [bf(2, 64, 3584), bf(5, 2, 64, 2048)]
     back = [bf(6, 2, 64, 1024), bf(2, 64, 1536)]
@@ -875,8 +922,7 @@
         scratch_shapes=[
             *rows, *rows, bf(PLEN, HD), bf(PLEN, HD),
             *there, *there, *there, *there,
-            bf(6, N_KV, 2, GROUP, 512), bf(N_KV, 2, GROUP, 384),
-            bf(6, N_KV, 2, GROUP, 512), bf(N_KV, 2, GROUP, 384),
+            bf(5, N_KV, 2, GROUP, 512), bf(6, N_KV, 2, GROUP, 512),
             bf(LANES, HD), bf(LANES, HD), bf(OWN, HD), bf(OWN, HD),
             bf(PLEN // KB, HD, KB),
             f32(PLEN + OWN, LANES), f32(PLEN + OWN, LANES),
@@ -884,8 +930,8 @@
             bf(6, N_KV, GROUP, 512), bf(N_KV, GROUP, 768),
             bf(6, N_KV, GROUP, 512), bf(N_KV, GROUP, 768),
             *back, *back, *back, *back, *home, *home,
-            sem((5, 2)), sem((4, 2)), sem((4, 2)), *hop, *hop, *head,
-            *head, *hop_back, *hop_back, sem((7, 2)), sem((7, 2)),
+            sem((4, 2)), sem((4,)), sem((4, 7)), sem((4, 7)), sem((5, 2)), sem((5, 2)), *hop, *hop,
+            sem((5, 7)), sem((5, 7)), *head, *hop_back, *hop_back, sem((7, 2)), sem((7, 2)),
         ],
         compiler_params=pltpu.CompilerParams(
             collective_id=0, has_side_effects=True, vmem_limit_bytes=VMEM_BYTES
@@ -894,6 +940,35 @@
     )(info, q, g, k, v, mats, mats_back, keys, values)
 
 
+def settled_kernel(*refs):
+    n = (len(refs) - 2) // 3
+    ins, outs, held = refs[:n], refs[n : 2 * n], refs[2 * n : 3 * n]
+    into, out_of = refs[-2], refs[-1]
+    first = [pltpu.make_async_copy(ins[i], held[i], into.at[i]) for i in range(n)]
+    then = [pltpu.make_async_copy(held[i], outs[i], out_of.at[i]) for i in range(n)]
+    for cp in first:
+        cp.start()
+    for i in range(n):
+        first[i].wait()
+        then[i].start()
+    for cp in then:
+        cp.wait()
+
+
+def settled(*arrays):
+    hbm = pl.BlockSpec(memory_space=pl.ANY)
+    return pl.pallas_call(
+        settled_kernel,
+        out_shape=[jax.ShapeDtypeStruct(a.shape, a.dtype) for a in arrays],
+        in_specs=[hbm] * len(arrays),
+        out_specs=[hbm] * len(arrays),
+        scratch_shapes=[pltpu.VMEM(a.shape, a.dtype) for a in arrays]
+        + [pltpu.SemaphoreType.DMA((len(arrays),))] * 2,
+        compiler_params=pltpu.CompilerParams(vmem_limit_bytes=VMEM_BYTES),
+        name="settled",
+    )(*arrays)
+
+
 def per_device(
     q_tokens, grad_tokens, roll_keys, roll_values, prompt_keys, prompt_values,
     slot_prompt, prompt_owner, roll_len, prompt_len,
@@ -903,8 +978,8 @@
 
     def direct():
         tokens = (jnp.transpose(a, (1, 0, 2)) for a in arrays)
-        gq, gk, gv, dkeys, dvalues = mega(
-            info, *tokens, mats, mats_back, prompt_keys, prompt_values
+        gq, gk, gv, dkeys, dvalues = settled(
+            *mega(info, *tokens, mats, mats_back, prompt_keys, prompt_values)
         )
         return (*(jnp.transpose(a, (1, 0, 2)) for a in (gq, gk, gv)), dkeys, dvalues)
 

time: 130 us -> 118 us (0.908)
  local copies, waits for them, and re-layouts: 6.24 us -> 0 us
  Pallas kernels: 122 us -> 116 us
    pallas_call x1, Pallas kernels: 119 us -> 109 us  [mega(): pl.pallas_call(mega_kernel, out_shape=[jax.ShapeDtypeStruct((3, SLOTS, 81...]
    unnamed x7 -> x0, local copies, waits for them, and re-layouts: 6.24 us -> none
    pallas_call x1 -> x2, Pallas kernels: 3.41 us -> 6.96 us  [the longest x1 3.85 us: route_tables(): pl.pallas_call(tables_kernel, out_shape=[jax.ShapeDtypeStruct((2, 10, 64,...]
where the time goes in v4:
time: 118 us
  Pallas kernels  116 us (98%)
    pallas_call x1, Pallas kernels, mega(): pl.pallas_call(mega_kernel, out_shape=[jax.ShapeDtypeStruct((3, SLOTS, 81...  109 us
    pallas_call x1, Pallas kernels, route_tables(): pl.pallas_call(tables_kernel, out_shape=[jax.ShapeDtypeStruct((2, 10, 64,...  3.85 us
    pallas_call x1, Pallas kernels, settled(): pl.pallas_call(settled_kernel, out_shape=[jax.ShapeDtypeStruct(a.shape, a...  3.11 us

profile of v4, /device:TPU:1, one launch (start us, length us, event | category | flops | bytes accessed | tf_op | source)
XLA Modules:
  0.0 118.1 jit_solution(3721496705458996293)
XLA Ops:
  0.6 0.6 pad_add_fusion.where
  1.2 3.9 %tables.1 = (bf16[2,10,64,64]{3,2,1,0:T(8,128)(2,1)}, bf16[2,4,64,64]{3,2,1,0:T(8,128)(2,1)}, s32[2]{0:T(128)S(1)}) custom-call(s32[2]{0:T(128)} %pad_add_fusion.where, s32[32]{0:T(128)} %owner.1, s32[32]{0:T(128)} %prompt_len.1, s32[1,1024]{1,0:T(1,128)} %bitcast.440, s32[1,1024]{1,0:T(1,128)} %bitcast.441), custom_call_target="tpu_custom_call" | custom-call | tf_op jit(solution)/shard_map/tables/pallas_call | solution.py:361
  5.1 112.7 %conditional.1 = (bf16[32,3,8192]{2,0,1:T(8,128)(2,1)}, bf16[32,3,1024]{2,0,1:T(8,128)(2,1)}, bf16[32,3,1024]{2,0,1:T(8,128)(2,1)}, bf16[2048,128]{1,0:T(8,128)(2,1)}, bf16[2048,128]{1,0:T(8,128)(2,1)}) conditional(s32[]{:T(128)} %bitcast.50, (s32[1024]{0:T(1024)}, s32[32]{0:T(128)}, bf16[32,3,8192]{2,0,1:T(8,128)(2,1)}, s32[1024]{0:T(1024)}, ...), branch_computations={%region_0.28_spmd, %region_23.29_spmd} | conditional | flops 1047797248 | bytes 241717472 | solution.py:986
  5.4 109.1 %mega.1 = (bf16[3,32,8192]{2,1,0:T(8,128)(2,1)}, bf16[3,32,1024]{2,1,0:T(8,128)(2,1)}, bf16[3,32,1024]{2,1,0:T(8,128)(2,1)}, bf16[2048,128]{1,0:T(8,128)(2,1)}, bf16[2048,128]{1,0:T(8,128)(2,1)}) custom-call(s32[2]{0:T(128)S(1)} %get-tuple-element.132.info, bf16[3,32,8192]{2,1,0:T(8,128)(2,1)} %bitcast.410, bf16[3,32,8192]{2,1,0:T(8,128)(2,1)} %bitcast.411, ...), custom_call_target="tpu_custom_call" | custom-call | tf_op jit(solution)/shard_map/cond/branch_1_fun/mega/pallas_call | solution.py:911
  114.4 3.1 %settled.1 = (bf16[3,32,8192]{2,1,0:T(8,128)(2,1)}, bf16[3,32,1024]{2,1,0:T(8,128)(2,1)}, bf16[3,32,1024]{2,1,0:T(8,128)(2,1)}, bf16[2048,128]{1,0:T(8,128)(2,1)}, bf16[2048,128]{1,0:T(8,128)(2,1)}) custom-call(bf16[3,32,8192]{2,1,0:T(8,128)(2,1)} %get-tuple-element.141.refs_0_, bf16[3,32,1024]{2,1,0:T(8,128)(2,1)} %get-tuple-element.142.refs_1_, ...), custom_call_target="tpu_custom_call" | custom-call | tf_op jit(solution)/shard_map/cond/branch_1_fun/settled/pallas_call | solution.py:960
